TPU v7x, 32 devices: a whole 2x2x4 slice. The times are simulated.
32 devices in a mesh: grp: 2 (over x), exp: 4 (over y, core), base: 4 (over z).
Axes of the slice: x: 2, y: 2, z: 4, core: 2. Of those that a mesh axis runs over, the one named last changes fastest.
Arguments:
- tokens: bfloat16 [512, 7168], P(('grp', 'exp'), 'base'), parts along dimension 0, may hold values from -6 to 6
- expert_ids: int32 [512, 8], P(('grp', 'exp')), parts along dimension 0, may hold values from 0 to 15, all different within a row; in each aligned block of 64 rows (0 to 63, 64 to 127, ...) at most 48 rows name the same one
- gate_q: int32 [512, 8], P(('grp', 'exp')), parts along dimension 0, may hold values from 1 to 65536
- importance: float32 [7168], P('base'), may hold values from 0.5 to 18
- dense_gate: bfloat16 [16, 7168, 1024], P('exp', None, 'base'), may hold values from -0.0625 to 0.0625
- dense_up: bfloat16 [16, 7168, 1024], P('exp', None, 'base'), may hold values from -0.0625 to 0.0625
- dense_down: bfloat16 [16, 1024, 7168], P('exp', None, 'base'), may hold values from -0.1875 to 0.1875
- delta_gate: bfloat16 [16, 7168, 128], P('exp', None, 'base'), may hold values from -0.0625 to 0.0625
- delta_up: bfloat16 [16, 7168, 128], P('exp', None, 'base'), may hold values from -0.0625 to 0.0625
- delta_down: bfloat16 [16, 128, 7168], P('exp', None, 'base'), may hold values from -0.5 to 0.5
- base_gate: bfloat16 [7168, 1024], P(None, 'base'), may hold values from -0.0625 to 0.0625
- base_up: bfloat16 [7168, 1024], P(None, 'base'), may hold values from -0.0625 to 0.0625
- base_down: bfloat16 [1024, 7168], P('base'), may hold values from -0.1875 to 0.1875
Outputs:
- errors: float32 [512], P(('grp', 'exp')), parts along dimension 0
There are 2 independent parts, one for each index of `grp`. A program takes and returns all parts, laid end to end along the dimension named above; an argument that names none is the same for every part. Nothing has to cross between parts.
Inputs may be any that keep to these rules, and one draw needn't show every extreme that they name: `expert_ids`: A token names 8 different experts; among the tokens of one index of exp no expert is named more than 48 times.
All inputs are finite; a program needn't handle non-finite values.
Results may differ from a plain program's by a relative error of at most 0.00064.
Values may be sent and summed in bfloat16 or wider, within the bound.
A program may use at most 256 MiB of HBM per device.

v0:
```python
import jax
import jax.numpy as jnp
from jax import lax
from jax.sharding import PartitionSpec as P

D = 7168


def shards(
    tokens,
    expert_ids,
    gate_q,
    importance,
    dense_gate,
    dense_up,
    dense_down,
    delta_gate,
    delta_up,
    delta_down,
    base_gate,
    base_up,
    base_down,
):
    groups = lax.axis_size("exp")
    splits = lax.axis_size("base")
    tok_rows, local_width = tokens.shape
    top_k = expert_ids.shape[1]
    local_experts = dense_gate.shape[0]
    experts_all = local_experts * groups
    capacity = tok_rows * top_k * 3 // (2 * experts_all)
    dense_width = dense_gate.shape[2]
    low_width = delta_gate.shape[2]
    flat_ids = expert_ids.reshape(-1)
    onehot = (flat_ids[:, None] == jnp.arange(experts_all, dtype=jnp.int32)[None, :]).astype(
        jnp.int32
    )
    position = jnp.sum((jnp.cumsum(onehot, axis=0) - onehot) * onehot, axis=1)
    flat_slot = flat_ids * capacity + position
    owners = jnp.arange(tok_rows * top_k, dtype=jnp.int32) // top_k
    slot_table = jnp.full((experts_all * capacity,), tok_rows, jnp.int32).at[flat_slot].set(owners)
    full_rows = lax.all_gather(tokens, "base", axis=1, tiled=True)
    base_cols = jnp.concatenate([base_gate, base_up], axis=1)
    base_pre = jnp.dot(full_rows, base_cols, preferred_element_type=jnp.float32)
    shared_width = base_gate.shape[1]
    shared = (jax.nn.silu(base_pre[:, :shared_width]) * base_pre[:, shared_width:]).astype(
        jnp.bfloat16
    )
    partial_value = jnp.dot(shared, base_down, preferred_element_type=jnp.float32)
    base_out = lax.psum_scatter(partial_value, "base", scatter_dimension=1, tiled=True).astype(
        jnp.bfloat16
    )
    base_out = lax.optimization_barrier(base_out)
    in_cols = jnp.concatenate([dense_gate, dense_up, delta_gate, delta_up], axis=2)
    dense_part = dense_down.reshape(local_experts, splits, dense_width, local_width)
    low_part = (-delta_down).reshape(local_experts, splits, low_width, local_width)
    down_rows = jnp.concatenate([dense_part, low_part], axis=2).reshape(
        local_experts, splits * (dense_width + low_width), local_width
    )
    source = jnp.concatenate(
        [full_rows, jnp.zeros((1, full_rows.shape[1]), full_rows.dtype)], axis=0
    )
    outgoing = source[slot_table].reshape(experts_all, capacity, full_rows.shape[1])
    arrived = lax.all_to_all(outgoing, "exp", split_axis=0, concat_axis=0, tiled=True)
    arrived = arrived.reshape(groups, local_experts, capacity, full_rows.shape[1])
    preacts = jnp.einsum("sjcd,jdh->sjch", arrived, in_cols, preferred_element_type=jnp.float32)
    gate_part = preacts[..., :dense_width]
    up_part = preacts[..., dense_width : 2 * dense_width]
    low_gate = preacts[..., 2 * dense_width : 2 * dense_width + low_width]
    low_up = preacts[..., 2 * dense_width + low_width :]
    hidden = (jax.nn.silu(gate_part) * up_part).astype(jnp.bfloat16)
    low_rank = (jax.nn.silu(low_gate) * low_up).astype(jnp.bfloat16)
    hidden = jnp.concatenate([hidden, low_rank], axis=3)
    residual = jnp.einsum(
        "sjch,jhd->sjcd",
        lax.all_gather(hidden, "base", axis=3, tiled=True),
        down_rows,
        preferred_element_type=jnp.float32,
    ).astype(jnp.bfloat16)
    residual = residual.reshape(groups * local_experts, capacity, local_width)
    weights_k = gate_q.astype(jnp.float32) / 65536.0
    returned = lax.all_to_all(residual, "exp", split_axis=0, concat_axis=0, tiled=True)
    picked = jnp.take(returned.reshape(experts_all * capacity, local_width), flat_slot, axis=0)
    picked = picked.reshape(tok_rows, top_k, local_width).astype(jnp.float32)
    deviation = picked - base_out.astype(jnp.float32)[:, None, :]
    squares = jnp.sum(importance * deviation * deviation, axis=2)
    partial_err = jnp.sum(weights_k * squares, axis=1) / D
    return lax.psum(partial_err, "base")


def solution(mesh):
    in_specs = (
        P(("grp", "exp"), "base"),
        P(("grp", "exp"), None),
        P(("grp", "exp"), None),
        P("base"),
        P("exp", None, "base"),
        P("exp", None, "base"),
        P("exp", None, "base"),
        P("exp", None, "base"),
        P("exp", None, "base"),
        P("exp", None, "base"),
        P(None, "base"),
        P(None, "base"),
        P("base", None),
    )
    out_specs = P(("grp", "exp"))
    return jax.shard_map(shards, mesh=mesh, in_specs=in_specs, out_specs=out_specs, check_vma=False)
```

profile of v0, /device:TPU:0, one launch (start us, length us, event | category | flops | bytes accessed | tf_op | source)
XLA Modules:
  0.0 351.0 jit_solution(7311459492607674761)
XLA Ops:
  6.5 0.8 copy.38
  7.3 0.1 eq.26
  7.4 0.1 reshape.103
  7.5 1.2 reduce-window.6
  8.7 0.2 slice_reduce_fusion
  8.9 0.1 mul.67
  9.0 0.1 fusion.34
  9.1 2.4 scatter_custom_fusion
  11.6 23.0 %all_gather.6 = bf16[64,7168]{1,0:T(8,128)(2,1)S(1)} all-gather(bf16[64,1792]{1,0:T(8,128)(2,1)} %param.13), channel_id=1, replica_groups=mesh['grp'=2,'exp'=4,'base'=4] {'base'}, dimensions={1}, use_global_device_ids=true | all-gather | bytes 1146880 | tf_op jit(solution)/shard_map/all_gather | solution.py:41
  34.6 0.1 concatenate.17
  34.7 9.4 %gather_fusion = bf16[768,7168]{1,0:T(8,128)(2,1)} fusion(bf16[65,7168]{1,0:T(8,128)(2,1)S(1)} %concatenate.17, s32[1024]{0:T(1024)S(1)} %pad_clamp_fusion.1), kind=kCustom, calls=%fused_computation | custom fusion | bytes 22023168 | tf_op jit(solution)/shard_map/gather | solution.py:62
  44.0 6.1 %all-to-all-start = ((bf16[16,48,7168]{2,1,0:T(8,128)(2,1)}), bf16[16,48,7168]{2,1,0:T(8,128)(2,1)}, u32[]{:S(2)}, u32[]{:S(2)}) async-start(bf16[16,48,7168]{2,1,0:T(8,128)(2,1)} %bitcast.56), calls=%async_computation | async-start | bytes 22020096 | tf_op jit(solution)/shard_map/all_to_all | solution.py:63
  50.1 0.0 all-gather.2.cloned.1.call-start
  50.1 18.6 %copy.42 = bf16[4,7168,256]{1,2,0:T(8,128)(2,1)} copy(bf16[4,7168,256]{2,1,0:T(8,128)(2,1)} %param.17) | data formatting | bytes 29360128 | tf_op args[4]
  68.7 18.8 %copy.43 = bf16[4,7168,256]{1,2,0:T(8,128)(2,1)} copy(bf16[4,7168,256]{2,1,0:T(8,128)(2,1)} %param.18) | data formatting | bytes 29360128 | tf_op args[5]
  87.5 83.9 %all-to-all-done = bf16[16,48,7168]{2,1,0:T(8,128)(2,1)} async-done(((bf16[16,48,7168]{2,1,0:T(8,128)(2,1)}), bf16[16,48,7168]{2,1,0:T(8,128)(2,1)}, u32[]{:S(2)}, u32[]{:S(2)}) %all-to-all-start) | async-done | bytes 11010080 | tf_op jit(solution)/shard_map/all_to_all | solution.py:63
  171.3 18.8 %fusion.21 = f32[4,4,48,576]{3,2,0,1:T(8,128)S(1)} fusion(bf16[4,4,48,7168]{3,2,1,0:T(8,128)(2,1)} %bitcast.11, bf16[4,7168,32]{1,2,0:T(8,128)(2,1)} %param.21, bf16[4,7168,32]{1,2,0:T(8,128)(2,1)} %param.20, bf16[4,7168,256]{1,2,0:T(8,128)(2,1)} %copy.43, bf16[4,7168,256]{1,2,0:T(8,128)(2,1)} %copy.42), kind=kOutput, calls=%fused_computation.24 | convolution fusion | flops 6473908224 | bytes 45809664 | tf_op jit(solution)/shard_map/sjcd,jdh->sjch/dot_general | solution.py:65
  190.1 0.2 fusion.27
  190.4 0.2 fusion.28
  190.6 0.1 pad_maximum_fusion.1
  190.6 1.6 copy.45
  192.3 0.0 all-gather.2.cloned.1.call-update
  192.3 0.0 reduce-scatter.2.cloned.1.call-start
  192.3 0.0 copy-start
  192.3 4.1 %fusion.24 = f32[64,512]{1,0:T(8,128)S(1)} fusion(bf16[64,7168]{1,0:T(8,128)(2,1)S(1)} %all_gather.6, bf16[7168,256]{1,0:T(8,128)(2,1)} %param.24, bf16[7168,256]{1,0:T(8,128)(2,1)} %param.23), kind=kOutput, calls=%fused_computation.25 | convolution fusion | flops 484442112 | bytes 8388608 | tf_op jit(solution)/shard_map/dot_general | solution.py:43
  196.4 0.1 copy-done
  196.5 0.0 copy-start.1
  196.5 2.0 fusion.30
  198.5 0.0 reduce-scatter.2.cloned.1.call-update
  198.6 0.0 copy-done.1
  198.6 0.3 neg.15
  198.9 13.2 %pad_maximum_fusion = bf16[4,4,288,1792]{3,2,1,0:T(8,128)(2,1)} fusion(bf16[4,4,32,1792]{3,2,1,0:T(8,128)(2,1)S(1)} %bitcast.60, bf16[4,4,256,1792]{3,2,1,0:T(8,128)(2,1)} %bitcast.58), kind=kLoop, calls=%fused_computation.11 | loop fusion | flops 33030144 | bytes 33030144 | tf_op jit(solution)/shard_map/concatenate | solution.py:56
  212.1 68.4 %all-gather.2.cloned.1.call-done = bf16[4,4,48,1152]{2,1,0,3:T(4,128)(2,1)} async-done(((bf16[4,4,48,288]{2,1,0,3:T(4,128)(2,1)}), bf16[4,4,48,1152]{2,1,0,3:T(4,128)(2,1)}) %all-gather.2.cloned.1.call-update) | async-done | bytes 1769488 | tf_op jit(solution)/shard_map/all_gather | solution.py:75
  280.5 10.3 %fusion.18 = bf16[4,4,48,1792]{3,2,0,1:T(8,128)(2,1)S(1)} fusion(bf16[4,1152,1792,1]{2,1,3,0:T(8,128)(2,1)} %bitcast.57, bf16[4,4,48,1152]{2,1,0,3:T(4,128)(2,1)} %all-gather.2.cloned.1.call-done), kind=kOutput, calls=%fused_computation.23 | convolution fusion | flops 3172270080 | bytes 21037056 | tf_op jit(solution)/shard_map/sjch,jhd->sjcd/dot_general | solution.py:73
  290.8 1.7 copy.47
  292.6 3.7 %all-to-all-start.1 = ((bf16[16,48,1792]{2,1,0:T(8,128)(2,1)}), bf16[16,48,1792]{2,1,0:T(8,128)(2,1)S(1)}, u32[]{:S(2)}, u32[]{:S(2)}) async-start(bf16[16,48,1792]{2,1,0:T(8,128)(2,1)} %bitcast.59), calls=%async_computation.1 | async-start | bytes 5505024 | tf_op jit(solution)/shard_map/all_to_all | solution.py:81
  296.3 0.1 reduce_sum.34
  296.4 0.1 broadcast_in_dim.23
  296.5 24.2 %reduce-scatter.2.cloned.1.call-done = f32[64,1792]{1,0:T(8,128)} async-done(((f32[64,7168]{1,0:T(8,128)}), f32[64,1792]{1,0:T(8,128)}) %reduce-scatter.2.cloned.1.call-update) | async-done | bytes 458768 | tf_op jit(solution)/shard_map/reduce_scatter | solution.py:49
  320.7 1.0 convert_element_type.46
  321.8 7.1 %all-to-all-done.1 = bf16[16,48,1792]{2,1,0:T(8,128)(2,1)S(1)} async-done(((bf16[16,48,1792]{2,1,0:T(8,128)(2,1)}), bf16[16,48,1792]{2,1,0:T(8,128)(2,1)S(1)}, u32[]{:S(2)}, u32[]{:S(2)}) %all-to-all-start.1) | async-done | bytes 2752544 | tf_op jit(solution)/shard_map/all_to_all | solution.py:81
  328.9 0.0 copy-start.2
  328.9 0.0 copy-start.3
  328.9 3.2 gather_fusion.1
  332.1 0.0 copy-done.2
  332.1 2.4 fusion.14
  334.5 0.1 reduce_sum.37
  334.6 0.1 copy.48
  334.6 0.0 copy-done.3
  334.7 9.4 %psum.7 = f32[64]{0:T(128)} all-reduce(f32[64]{0:T(128)S(1)} %broadcast_multiply_fusion.1), channel_id=1, replica_groups=mesh['grp'=2,'exp'=4,'base'=4] {'base'}, use_global_device_ids=true, to_apply=%region_7.8 | all-reduce | flops 64 | bytes 512 | tf_op jit(solution)/shard_map/psum | solution.py:87
  (13 shorter events, 0.2 us)
Async XLA Ops:
  44.0 127.3 %all-to-all-start = ((bf16[16,48,7168]{2,1,0:T(8,128)(2,1)}), bf16[16,48,7168]{2,1,0:T(8,128)(2,1)}, u32[]{:S(2)}, u32[]{:S(2)}) async-start(bf16[16,48,7168]{2,1,0:T(8,128)(2,1)} %bitcast.56), calls=%async_computation | async-start | bytes 22020096 | tf_op jit(solution)/shard_map/all_to_all | solution.py:63
  50.1 230.4 %all-gather.2.cloned.1.call-start = ((), (), s32[]{:S(2)}) async-start(), calls=%async_computation.3 | async-start | bytes 5898240 | tf_op jit(solution)/shard_map/all_gather | solution.py:75
  192.3 128.5 %reduce-scatter.2.cloned.1.call-start = ((), (), s32[]{:S(2)}) async-start(), calls=%async_computation.4 | async-start | bytes 2293760 | tf_op jit(solution)/shard_map/reduce_scatter | solution.py:49
  192.3 4.2 %copy-start = (bf16[256,7168]{1,0:T(8,128)(2,1)S(1)}, bf16[256,7168]{1,0:T(8,128)(2,1)}, u32[]{:S(2)}) copy-start(bf16[256,7168]{1,0:T(8,128)(2,1)} %param.25) | copy-start | bytes 11010052
  196.5 2.0 copy-start.1
  292.6 36.4 %all-to-all-start.1 = ((bf16[16,48,1792]{2,1,0:T(8,128)(2,1)}), bf16[16,48,1792]{2,1,0:T(8,128)(2,1)S(1)}, u32[]{:S(2)}, u32[]{:S(2)}) async-start(bf16[16,48,1792]{2,1,0:T(8,128)(2,1)} %bitcast.59), calls=%async_computation.1 | async-start | bytes 5505024 | tf_op jit(solution)/shard_map/all_to_all | solution.py:81
  328.9 3.2 copy-start.2
  328.9 5.7 %copy-start.3 = (s32[64,8]{0,1:T(8,128)S(1)}, s32[64,8]{0,1:T(8,128)}, u32[]{:S(2)}) copy-start(s32[64,8]{0,1:T(8,128)} %param.15) | copy-start | bytes 6148
Sparse Core Ops, SparseCore 0:
  192.4 88.0 all-gather.1
  282.8 37.8 reduce-scatter.1
where the time goes:
time: 352 us; the launch traced here: 351 us
  waiting for transfers between devices  184 us (52%)
  local copies, waits for them, and re-layouts  57.5 us (16%)
  matrix products  35.2 us (10%)
  blocking collectives  32.4 us (9%)
  other arithmetic  18.8 us (5%)
  between operations  13.6 us (4%)
  starting transfers between devices  9.82 us (3%)
    all_to_all x1, waiting for transfers between devices, shards(): lax.all_to_all(outgoing, 'exp', split_axis=0, concat_axis=0, tiled=True)  83.9 us
    all_gather x1, waiting for transfers between devices, shards(): lax.all_gather(hidden, 'base', axis=3, tiled=True)  68.4 us
    unnamed x11, local copies, waits for them, and re-layouts  38.2 us
    reduce_scatter x1, waiting for transfers between devices, shards(): lax.psum_scatter(partial_value, 'base', scatter_dimension=1, tiled=True)  24.2 us
    all_gather x1, blocking collectives, shards(): full_rows = lax.all_gather(tokens, 'base', axis=1, tiled=True)  23 us
    dot_general x1, matrix products, shards(): jnp.einsum('sjcd,jdh->sjch', arrived, in_cols, preferred_element_type=jnp...  18.8 us
    concatenate x1, other arithmetic, shards(): jnp.concatenate([dense_part, low_part], axis=2)  13.2 us
    dot_general x1, matrix products, shards(): jnp.einsum('sjch,jhd->sjcd', lax.all_gather(hidden, 'base', axis=3, tiled...  10.3 us
  transfers between devices with their start and end apart: 4, of which 4 were waited for; matrix products, arithmetic and copies ran while one was open for 20% of the time, Pallas kernels for 0%

commit v1 on v0

v1 whole, which is shorter than its diff:
```python
import jax
import jax.numpy as jnp
from jax import lax
from jax.sharding import PartitionSpec as P

D = 7168


def swiglu(rows, gate_w, up_w):
    gate_pre = jnp.dot(rows, gate_w, preferred_element_type=jnp.float32)
    up_pre = jnp.dot(rows, up_w, preferred_element_type=jnp.float32)
    return (jax.nn.silu(gate_pre) * up_pre).astype(jnp.bfloat16)


def shards(
    tokens,
    expert_ids,
    gate_q,
    importance,
    dense_gate,
    dense_up,
    dense_down,
    delta_gate,
    delta_up,
    delta_down,
    base_gate,
    base_up,
    base_down,
):
    groups = lax.axis_size("exp")
    splits = lax.axis_size("base")
    tok_rows, local_width = tokens.shape
    top_k = expert_ids.shape[1]
    local_experts = dense_gate.shape[0]
    capacity = tok_rows * top_k * 3 // (2 * local_experts * groups)
    dense_width = dense_gate.shape[2]
    low_width = delta_gate.shape[2]
    all_rows = tok_rows * groups
    slots = capacity * groups

    routing = lax.all_gather(
        jnp.concatenate([expert_ids, gate_q], axis=1), "exp", axis=0, tiled=True
    )
    own_rows = lax.all_gather(tokens, "base", axis=1, tiled=True)
    rows = lax.all_gather(own_rows, "exp", axis=0, tiled=True)

    ids, gates = routing[:, :top_k], routing[:, top_k:]
    first = lax.axis_index("exp") * local_experts
    mine = first + jnp.arange(local_experts, dtype=jnp.int32)
    hit = ids[:, None, :] == mine[None, :, None]
    weight = jnp.sum(jnp.where(hit, gates[:, None, :].astype(jnp.float32), 0.0), axis=2) / 65536.0
    named = jnp.any(hit, axis=2)
    order = jnp.arange(all_rows, dtype=jnp.int32)
    block = order // tok_rows
    before = (block[:, None] == block[None, :]) & (order[None, :] < order[:, None])
    position = jnp.dot(
        before.astype(jnp.bfloat16), named.astype(jnp.bfloat16), preferred_element_type=jnp.float32
    ).astype(jnp.int32)
    slot = jnp.where(named, block[:, None] * capacity + position, -1)
    pick = jnp.arange(slots, dtype=jnp.int32)[None, :, None] == slot.T[:, None, :]
    select = pick.astype(jnp.bfloat16)

    shared = swiglu(own_rows, base_gate, base_up)
    partial_value = jnp.dot(shared, base_down, preferred_element_type=jnp.float32)
    base_own = lax.psum_scatter(
        partial_value.astype(jnp.bfloat16), "base", scatter_dimension=1, tiled=True
    )
    base_all = lax.all_gather(base_own, "exp", axis=0, tiled=True)

    packed = []
    for j in range(local_experts):
        hidden = swiglu(rows, dense_gate[j], dense_up[j])
        low = swiglu(rows, delta_gate[j], delta_up[j])
        both = jnp.concatenate([hidden, low], axis=1)
        packed.append(
            jnp.dot(select[j], both, preferred_element_type=jnp.float32).astype(jnp.bfloat16)
        )
    sent = jnp.stack(packed)
    full = lax.all_gather(sent, "base", axis=0, tiled=False)

    total = jnp.zeros((all_rows,), jnp.float32)
    for j in range(local_experts):
        hid = jnp.concatenate([full[b, j, :, :dense_width] for b in range(splits)], axis=1)
        low = jnp.concatenate([full[b, j, :, dense_width:] for b in range(splits)], axis=1)
        residual = jnp.dot(hid, dense_down[j], preferred_element_type=jnp.float32) - jnp.dot(
            low, delta_down[j], preferred_element_type=jnp.float32
        )
        residual = residual.astype(jnp.bfloat16).astype(jnp.float32)
        base_rows = jnp.dot(select[j], base_all, preferred_element_type=jnp.float32)
        deviation = residual - base_rows
        squares = jnp.sum(importance * deviation * deviation, axis=1)
        back = jnp.sum(jnp.where(pick[j], squares[:, None], 0.0), axis=0)
        total = total + weight[:, j] * back
    total = lax.psum(total / D, ("exp", "base"))
    return lax.dynamic_slice_in_dim(total, lax.axis_index("exp") * tok_rows, tok_rows)


def solution(mesh):
    in_specs = (
        P(("grp", "exp"), "base"),
        P(("grp", "exp"), None),
        P(("grp", "exp"), None),
        P("base"),
        P("exp", None, "base"),
        P("exp", None, "base"),
        P("exp", None, "base"),
        P("exp", None, "base"),
        P("exp", None, "base"),
        P("exp", None, "base"),
        P(None, "base"),
        P(None, "base"),
        P("base", None),
    )
    out_specs = P(("grp", "exp"))
    return jax.shard_map(shards, mesh=mesh, in_specs=in_specs, out_specs=out_specs, check_vma=False)
```

time: 352 us -> 205 us (0.58)
  waiting for transfers between devices: 184 us -> 55.4 us
  local copies, waits for them, and re-layouts: 57.5 us -> 3.8 us
  blocking collectives: 32.4 us -> 70 us
  matrix products: 35.2 us -> 58.1 us
  other arithmetic: 18.8 us -> 1.49 us
  starting transfers between devices: 9.82 us -> 0.09 us
    all_to_all x2 -> x0, waiting for transfers between devices: 91 us -> none  [the longest x1 83.9 us: shards(): lax.all_to_all(outgoing, 'exp', split_axis=0, concat_axis=0, tiled=True)]
    unnamed x11 -> x33, local copies, waits for them, and re-layouts: 38.2 us -> 0.31 us
    reduce_scatter x1, waiting for transfers between devices: 24.2 us -> 0.03 us  [shards(): lax.psum_scatter(partial_value.astype(jnp.bfloat16), 'base', scatter_dime...]
    psum x1, blocking collectives: 9.42 us -> 31.3 us  [shards(): total = lax.psum(total / D, ('exp', 'base'))]
    dot_general x3 -> x34, matrix products: 33.1 us -> 51.4 us  [the longest x8 20.1 us: swiglu(): up_pre = jnp.dot(rows, up_w, preferred_element_type=jnp.float32)]
    all_gather x1 -> x3, blocking collectives: 23 us -> 38.7 us  [the longest x1 23.4 us: shards(): own_rows = lax.all_gather(tokens, 'base', axis=1, tiled=True)]
    concatenate x2 -> x0, other arithmetic: 13.3 us -> none  [the longest x1 13.2 us: shards(): jnp.concatenate([dense_part, low_part], axis=2)]
    all_gather x1 -> x2, waiting for transfers between devices: 68.4 us -> 55.4 us  [the longest x1 40.2 us: shards(): full = lax.all_gather(sent, 'base', axis=0, tiled=False)]
  transfers between devices with their start and end apart: 4 -> 3, of which waited for: 4 -> 2; matrix products, arithmetic and copies ran while one was open for 20% -> 24% of each run, Pallas kernels for 0% -> 0%
where the time goes in v1:
time: 205 us; the launch traced here: 204 us
  blocking collectives  70 us (34%)
  matrix products  58.1 us (28%)
  waiting for transfers between devices  55.4 us (27%)
  between operations  15.3 us (7%)
  local copies, waits for them, and re-layouts  3.8 us (2%)
    all_gather x1, waiting for transfers between devices, shards(): full = lax.all_gather(sent, 'base', axis=0, tiled=False)  40.2 us
    psum x1, blocking collectives, shards(): total = lax.psum(total / D, ('exp', 'base'))  31.3 us
    all_gather x1, blocking collectives, shards(): own_rows = lax.all_gather(tokens, 'base', axis=1, tiled=True)  23.4 us
    dot_general x8, matrix products, swiglu(): up_pre = jnp.dot(rows, up_w, preferred_element_type=jnp.float32)  20.1 us
    dot_general x9, matrix products, swiglu(): gate_pre = jnp.dot(rows, gate_w, preferred_element_type=jnp.float32)  18.7 us
    all_gather x1, waiting for transfers between devices, shards(): rows = lax.all_gather(own_rows, 'exp', axis=0, tiled=True)  15.2 us
    all_gather x1, blocking collectives, shards(): base_all = lax.all_gather(base_own, 'exp', axis=0, tiled=True)  9.8 us
    dot_general x4, matrix products, shards(): jnp.dot(hid, dense_down[j], preferred_element_type=jnp.float32)  7.97 us
  transfers between devices with their start and end apart: 3, of which 2 were waited for; matrix products, arithmetic and copies ran while one was open for 24% of the time, Pallas kernels for 0%

profile of v1, /device:TPU:0, one launch (start us, length us, event | category | flops | bytes accessed | tf_op | source)
XLA Modules:
  0.0 204.3 jit_solution(16887898204992520157)
XLA Ops:
  7.4 23.4 %all_gather.19 = bf16[64,7168]{1,0:T(8,128)(2,1)} all-gather(bf16[64,1792]{1,0:T(8,128)(2,1)} %param.13), channel_id=1, replica_groups=mesh['grp'=2,'exp'=4,'base'=4] {'base'}, dimensions={1}, use_global_device_ids=true | all-gather | bytes 1146880 | tf_op jit(solution)/shard_map/all_gather | solution.py:44
  30.8 0.0 all-gather.5.cloned.1.call-update
  30.8 0.0 reduce-scatter.2.cloned.1.call-start
  30.9 3.1 %fusion.206 = f32[64,256]{1,0:T(8,128)S(1)} fusion(bf16[64,7168]{1,0:T(8,128)(2,1)} %all_gather.19, bf16[7168,256]{1,0:T(8,128)(2,1)} %param.23), kind=kOutput, calls=%fused_computation.267 | convolution fusion | flops 234881024 | bytes 4653056 | tf_op jit(solution)/shard_map/dot_general | solution.py:10
  34.0 6.8 %convolution_convert_fusion = bf16[64,7168]{1,0:T(8,128)(2,1)} fusion(bf16[256,7168]{1,0:T(8,128)(2,1)} %param.25, bf16[64,7168]{1,0:T(8,128)(2,1)S(1)} %copy-done.1, bf16[7168,256]{1,0:T(8,128)(2,1)} %param.24, f32[64,256]{1,0:T(8,128)S(1)} %fusion.206), kind=kOutput, calls=%fused_computation | convolution fusion | flops 470319104 | bytes 9240576 | tf_op jit(solution)/shard_map/dot_general | solution.py:64
  40.8 0.0 reduce-scatter.2.cloned.1.call-update
  40.8 0.0 all-gather.7.cloned.1.call-start
  40.9 5.5 %all-gather.1 = s32[4,64,16]{1,2,0:T(8,128)S(1)} all-gather(s32[1,64,16]{1,2,0:T(8,128)S(1)} %add_bitcast_fusion), channel_id=1, replica_groups=mesh['grp'=2,'exp'=4,'base'=4] {'exp'}, dimensions={0}, use_global_device_ids=true | all-gather | bytes 20480 | tf_op jit(solution)/shard_map/all_gather | solution.py:41
  46.4 0.1 reshape.45
  46.5 0.1 compare_reduce_fusion
  46.6 0.2 fusion.82
  46.9 0.1 iota_compare_fusion
  47.0 15.2 %all-gather.5.cloned.1.call-done = bf16[256,7168]{1,0:T(8,128)(2,1)} async-done(((bf16[64,7168]{1,0:T(8,128)(2,1)}), bf16[256,7168]{1,0:T(8,128)(2,1)}) %all-gather.5.cloned.1.call-update) | async-done | bytes 3670032 | tf_op jit(solution)/shard_map/all_gather | solution.py:45
  62.2 3.4 %fusion.88 = f32[256,32]{0,1:T(8,128)S(1)} fusion(bf16[256,7168]{1,0:T(8,128)(2,1)} %all-gather.5.cloned.1.call-done, bf16[4,7168,32]{1,2,0:T(8,128)(2,1)S(1)} %copy-done.2), kind=kOutput, calls=%fused_computation.97 | convolution fusion | flops 117440512 | bytes 4161536 | tf_op jit(solution)/shard_map/dot_general | solution.py:10
  65.6 0.0 copy-done
  65.6 3.8 %fusion.10 = f32[256,256]{0,1:T(8,128)S(1)} fusion(bf16[256,7168]{1,0:T(8,128)(2,1)S(1)} %copy-done, bf16[4,7168,256]{2,1,0:T(8,128)(2,1)} %param.17), kind=kOutput, calls=%fused_computation.11 | convolution fusion | flops 939524096 | bytes 7602176 | tf_op jit(solution)/shard_map/dot_general | solution.py:10
  69.5 1.2 fusion.80
  70.7 0.0 slice-start.1
  70.7 3.9 %fusion.60 = bf16[256,256]{0,1:T(8,128)(2,1)S(1)} fusion(bf16[256,7168]{1,0:T(8,128)(2,1)S(1)} %copy-done, bf16[4,7168,256]{2,1,0:T(8,128)(2,1)} %param.18, f32[256,256]{0,1:T(8,128)S(1)} %fusion.10), kind=kOutput, calls=%fused_computation.69 | convolution fusion | flops 939917312 | bytes 7733248 | tf_op jit(solution)/shard_map/dot_general | solution.py:11
  74.6 0.2 fusion.75
  74.8 1.2 fusion.91
  76.0 0.0 slice-start.3
  76.0 1.2 fusion.94
  77.2 1.2 fusion.97
  78.4 0.0 slice-done
  78.5 1.6 fusion.14
  80.1 1.6 fusion.18
  81.7 1.2 fusion.79
  82.9 1.2 fusion.78
  84.2 3.9 %fusion.63 = bf16[256,256]{0,1:T(8,128)(2,1)S(1)} fusion(bf16[256,7168]{1,0:T(8,128)(2,1)S(1)} %copy-done, bf16[4,7168,256]{2,1,0:T(8,128)(2,1)} %param.18, f32[256,256]{0,1:T(8,128)S(1)} %fusion.14), kind=kOutput, calls=%fused_computation.70 | convolution fusion | flops 939917312 | bytes 7733248 | tf_op jit(solution)/shard_map/dot_general | solution.py:11
  88.1 3.7 %fusion.66 = bf16[256,256]{0,1:T(8,128)(2,1)S(1)} fusion(bf16[256,7168]{1,0:T(8,128)(2,1)S(1)} %copy-done, bf16[4,7168,256]{2,1,0:T(8,128)(2,1)} %param.18, f32[256,256]{0,1:T(8,128)S(1)} %fusion.18), kind=kOutput, calls=%fused_computation.71 | convolution fusion | flops 939917312 | bytes 7733248 | tf_op jit(solution)/shard_map/dot_general | solution.py:11
  91.8 0.2 fusion.74
  92.1 0.2 fusion.73
  92.3 1.2 fusion.77
  93.5 1.6 fusion.22
  95.1 3.7 %fusion.69 = bf16[256,256]{0,1:T(8,128)(2,1)S(1)} fusion(bf16[256,7168]{1,0:T(8,128)(2,1)S(1)} %copy-done, bf16[4,7168,256]{2,1,0:T(8,128)(2,1)} %param.18, f32[256,256]{0,1:T(8,128)S(1)} %fusion.22), kind=kOutput, calls=%fused_computation.72 | convolution fusion | flops 939917312 | bytes 7733248 | tf_op jit(solution)/shard_map/dot_general | solution.py:11
  98.9 0.2 fusion.72
  99.1 0.9 pad_maximum_fusion
  100.0 0.0 all-gather.7.cloned.1.call-update
  100.1 0.1 fusion.189
  100.2 0.0 reduce-scatter.2.cloned.1.call-done
  100.2 9.8 %all_gather.23 = bf16[256,1792]{1,0:T(8,128)(2,1)S(1)} all-gather(bf16[64,1792]{1,0:T(8,128)(2,1)} %reduce-scatter.2.cloned.1.call-done), channel_id=1, replica_groups=mesh['grp'=2,'exp'=4,'base'=4] {'exp'}, dimensions={0}, use_global_device_ids=true | all-gather | bytes 1146880 | tf_op jit(solution)/shard_map/all_gather | solution.py:68
  110.0 40.2 %all-gather.7.cloned.1.call-done = bf16[16,192,288]{2,1,0:T(8,128)(2,1)} async-done(((bf16[4,192,288]{2,1,0:T(8,128)(2,1)}), bf16[16,192,288]{2,1,0:T(8,128)(2,1)}) %all-gather.7.cloned.1.call-update) | async-done | bytes 1769488 | tf_op jit(solution)/shard_map/all_gather | solution.py:79
  150.2 1.2 slice_bitcast_fusion.39
  151.4 0.0 slice-start.4
  151.4 1.7 slice_bitcast_fusion.23
  153.1 0.0 slice-start.5
  153.1 3.1 %fusion.4 = f32[192,1792]{1,0:T(8,128)S(1)} fusion(bf16[4,1024,1792]{2,1,0:T(8,128)(2,1)} %param.19, bf16[192,256]{1,0:T(8,128)(2,1)S(1)} %get-tuple-element.34, bf16[192,256]{1,0:T(8,128)(2,1)S(1)} %get-tuple-element.35, bf16[192,256]{1,0:T(8,128)(2,1)S(1)} %get-tuple-element.36, bf16[192,256]{1,0:T(8,128)(2,1)S(1)} %get-tuple-element.25), kind=kOutput, calls=%fused_computation.5 | convolution fusion | flops 706215936 | bytes 5439488 | tf_op jit(solution)/shard_map/dot_general | solution.py:85
  156.2 0.4 fusion.39
  156.6 0.0 slice-start.6
  156.7 0.5 fusion.45
  157.1 3.1 %fusion = f32[192,1792]{1,0:T(8,128)S(1)} fusion(bf16[4,1024,1792]{2,1,0:T(8,128)(2,1)} %param.19, bf16[192,256]{1,0:T(8,128)(2,1)S(1)} %get-tuple-element.26, bf16[192,256]{1,0:T(8,128)(2,1)S(1)} %get-tuple-element.27, bf16[192,256]{1,0:T(8,128)(2,1)S(1)} %get-tuple-element.28, bf16[192,256]{1,0:T(8,128)(2,1)S(1)} %get-tuple-element.29), kind=kOutput, calls=%fused_computation.1 | convolution fusion | flops 706215936 | bytes 5439488 | tf_op jit(solution)/shard_map/dot_general | solution.py:85
  160.3 0.4 fusion.43
  160.7 0.5 fusion.47
  161.2 0.1 slice-done.7
  161.2 0.9 fusion.2
  162.1 0.4 fusion.41
  162.5 0.5 fusion.46
  163.0 0.9 fusion.6
  163.9 0.4 fusion.37
  164.3 0.5 fusion.44
  164.7 0.2 select_reduce_fusion.3
  165.0 31.3 %psum.7 = f32[256]{0:T(256)S(1)} all-reduce(f32[256]{0:T(256)S(1)} %add_multiply_fusion), channel_id=1, replica_groups=mesh['grp'=2,'exp'=4,'base'=4] {'exp','base'}, use_global_device_ids=true, to_apply=%region_11.12 | all-reduce | flops 256 | bytes 2048 | tf_op jit(solution)/shard_map/psum | solution.py:94
  196.3 0.6 dynamic_slice.3
  (35 shorter events, 0.1 us)
Async XLA Ops:
  7.4 54.8 %all-gather.5.cloned.1.call-start = ((), (), s32[]{:S(2)}) async-start(), calls=%async_computation.1 | async-start | bytes 4587520 | tf_op jit(solution)/shard_map/all_gather | solution.py:45
  30.8 3.2 %copy-start.1 = (bf16[64,7168]{1,0:T(8,128)(2,1)S(1)}, bf16[64,7168]{1,0:T(8,128)(2,1)}, u32[]{:S(2)}) copy-start(bf16[64,7168]{1,0:T(8,128)(2,1)} %all_gather.19) | copy-start | bytes 2752516
  30.8 69.4 %reduce-scatter.2.cloned.1.call-start = ((), (), s32[]{:S(2)}) async-start(), calls=%async_computation.2 | async-start | bytes 1146880 | tf_op jit(solution)/shard_map/reduce_scatter | solution.py:65
  34.0 6.9 %copy-start.6 = (s32[64,8]{0,1:T(8,128)S(1)}, s32[64,8]{0,1:T(8,128)}, u32[]{:S(2)}) copy-start(s32[64,8]{0,1:T(8,128)} %param.15) | copy-start | bytes 6148
  34.0 6.9 %copy-start.7 = (s32[64,8]{0,1:T(8,128)S(1)}, s32[64,8]{0,1:T(8,128)}, u32[]{:S(2)}) copy-start(s32[64,8]{0,1:T(8,128)} %param.14) | copy-start | bytes 6148
  34.0 28.2 %copy-start.2 = (bf16[4,7168,32]{1,2,0:T(8,128)(2,1)S(1)}, bf16[4,7168,32]{1,2,0:T(8,128)(2,1)}, u32[]{:S(2)}) copy-start(bf16[4,7168,32]{1,2,0:T(8,128)(2,1)} %param.20) | copy-start | bytes 5505028
  40.8 109.4 %all-gather.7.cloned.1.call-start = ((), (), s32[]{:S(2)}) async-start(), calls=%async_computation.3 | async-start | bytes 2949120 | tf_op jit(solution)/shard_map/all_gather | solution.py:79
  62.2 3.4 %copy-start = (bf16[256,7168]{1,0:T(8,128)(2,1)S(1)}, bf16[256,7168]{1,0:T(8,128)(2,1)}, u32[]{:S(2)}) copy-start(bf16[256,7168]{1,0:T(8,128)(2,1)} %all-gather.5.cloned.1.call-done) | copy-start | bytes 11010052
  65.6 3.8 %copy-start.3 = (bf16[4,7168,32]{1,2,0:T(8,128)(2,1)S(1)}, bf16[4,7168,32]{1,2,0:T(8,128)(2,1)}, u32[]{:S(2)}) copy-start(bf16[4,7168,32]{1,2,0:T(8,128)(2,1)} %param.21) | copy-start | bytes 5505028
  69.5 9.0 %slice-start = ((s8[14680064]{0:T(1024)(128)(4,1)}), s8[4194304]{0:T(1024)(128)(4,1)S(1)}, s32[]{:S(2)}) async-start(s8[14680064]{0:T(1024)(128)(4,1)} %bitcast.227), calls=%async_computation.4 | async-start | bytes 8388608
  70.7 7.8 %slice-start.1 = ((s8[14680064]{0:T(1024)(128)(4,1)}), s8[4194304]{0:T(1024)(128)(4,1)S(1)}, s32[]{:S(2)}) async-start(s8[14680064]{0:T(1024)(128)(4,1)} %bitcast.227), calls=%async_computation.5 | async-start | bytes 8388608
  70.7 7.8 %slice-start.2 = ((s8[14680064]{0:T(1024)(128)(4,1)}), s8[4194304]{0:T(1024)(128)(4,1)S(1)}, s32[]{:S(2)}) async-start(s8[14680064]{0:T(1024)(128)(4,1)} %bitcast.227), calls=%async_computation.6 | async-start | bytes 8388608
  76.0 2.5 %slice-start.3 = ((s8[14680064]{0:T(1024)(128)(4,1)}), s8[2097152]{0:T(1024)(128)(4,1)S(1)}, s32[]{:S(2)}) async-start(s8[14680064]{0:T(1024)(128)(4,1)} %bitcast.227), calls=%async_computation.7 | async-start | bytes 4194304
  151.4 9.8 %slice-start.4 = ((s8[14680064]{0:T(1024)(128)(4,1)}), s8[2097152]{0:T(1024)(128)(4,1)S(1)}, s32[]{:S(2)}) async-start(s8[14680064]{0:T(1024)(128)(4,1)} %bitcast.229), calls=%async_computation.8 | async-start | bytes 4194304
  153.1 3.1 %copy-start.4 = (bf16[4,128,1792]{2,1,0:T(8,128)(2,1)S(1)}, bf16[4,128,1792]{2,1,0:T(8,128)(2,1)}, u32[]{:S(2)}) copy-start(bf16[4,128,1792]{2,1,0:T(8,128)(2,1)} %param.22) | copy-start | bytes 5505028
  153.1 3.5 %copy-start.5 = (f32[1792]{0:T(1024)S(1)}, f32[1792]{0:T(1024)}, u32[]{:S(2)}) copy-start(f32[1792]{0:T(1024)} %param.16) | copy-start | bytes 21508
  153.1 8.0 %slice-start.5 = ((s8[14680064]{0:T(1024)(128)(4,1)}), s8[4194304]{0:T(1024)(128)(4,1)S(1)}, s32[]{:S(2)}) async-start(s8[14680064]{0:T(1024)(128)(4,1)} %bitcast.229), calls=%async_computation.9 | async-start | bytes 8388608
  156.6 4.5 %slice-start.6 = ((s8[14680064]{0:T(1024)(128)(4,1)}), s8[4194304]{0:T(1024)(128)(4,1)S(1)}, s32[]{:S(2)}) async-start(s8[14680064]{0:T(1024)(128)(4,1)} %bitcast.229), calls=%async_computation.10 | async-start | bytes 8388608
  157.1 4.1 %slice-start.7 = ((s8[14680064]{0:T(1024)(128)(4,1)}), s8[4194304]{0:T(1024)(128)(4,1)S(1)}, s32[]{:S(2)}) async-start(s8[14680064]{0:T(1024)(128)(4,1)} %bitcast.229), calls=%async_computation.11 | async-start | bytes 8388608
Sparse Core Ops, SparseCore 0:
  30.9 31.2 all-gather.4
Sparse Core Ops, SparseCore 1:
  40.9 24.4 reduce-scatter.1
  100.1 50.0 all-gather.6

commit v2 on v1

--- a/solution.py
+++ b/solution.py
@@ -1,9 +1,82 @@
+import functools
+
 import jax
 import jax.numpy as jnp
 from jax import lax
+from jax.experimental import pallas as pl
+from jax.experimental.pallas import tpu as pltpu
 from jax.sharding import PartitionSpec as P
 
 D = 7168
+
+
+def sum_kernel(groups, splits, part_ref, out_ref, held, send_sem, recv_sem):
+    n = groups * splits
+    mine = lax.axis_index("exp")
+    me = mine * splits + lax.axis_index("base")
+
+    def where(off):
+        peer = lax.rem(me + off, n)
+        return peer, {"exp": peer // splits, "base": lax.rem(peer, splits)}
+
+    barrier = pltpu.get_barrier_semaphore()
+
+    @pl.loop(1, n)
+    def _(off):
+        pl.semaphore_signal(
+            barrier, inc=1, device_id=where(off)[1], device_id_type=pl.DeviceIdType.MESH
+        )
+
+    pl.semaphore_wait(barrier, n - 1)
+
+    def copy(block, slot, off, device):
+        return pltpu.make_async_remote_copy(
+            src_ref=part_ref.at[block],
+            dst_ref=held.at[slot],
+            send_sem=send_sem.at[off],
+            recv_sem=recv_sem.at[slot],
+            device_id=device,
+            device_id_type=pl.DeviceIdType.MESH,
+        )
+
+    @pl.loop(1, n)
+    def _(off):
+        device = where(off)[1]
+        copy(device["exp"], me, off, device).start()
+
+    held[me] = part_ref[mine]
+
+    @pl.loop(1, n)
+    def _(off):
+        peer, device = where(off)
+        arrived = copy(mine, peer, off, device)
+        arrived.wait_recv()
+        arrived.wait_send()
+
+    total = held[0]
+    for source in range(1, n):
+        total = total + held[source]
+    out_ref[...] = total
+
+
+def sum_over_group(total, groups, splits):
+    tok_rows = total.shape[0] // groups
+    lanes = -(-tok_rows // 128) * 128
+    n = groups * splits
+    part = jnp.pad(total.reshape(groups, 1, tok_rows), ((0, 0), (0, 7), (0, lanes - tok_rows)))
+    out = pl.pallas_call(
+        functools.partial(sum_kernel, groups, splits),
+        out_shape=jax.ShapeDtypeStruct((8, lanes), jnp.float32),
+        in_specs=[pl.BlockSpec(memory_space=pltpu.VMEM)],
+        out_specs=pl.BlockSpec(memory_space=pltpu.VMEM),
+        scratch_shapes=[
+            pltpu.VMEM((n, 8, lanes), jnp.float32),
+            pltpu.SemaphoreType.DMA((n,)),
+            pltpu.SemaphoreType.DMA((n,)),
+        ],
+        compiler_params=pltpu.CompilerParams(collective_id=0, has_side_effects=True),
+    )(part)
+    return out[0, :tok_rows]
 
 
 def swiglu(rows, gate_w, up_w):
@@ -67,10 +140,17 @@
     )
     base_all = lax.all_gather(base_own, "exp", axis=0, tiled=True)
 
+    contract = (((1,), (1,)), ((), ()))
+    low_gates = delta_gate.transpose(0, 2, 1).reshape(local_experts * low_width, -1)
+    low_ups = delta_up.transpose(0, 2, 1).reshape(local_experts * low_width, -1)
+    low_pre = lax.dot_general(rows, low_gates, contract, preferred_element_type=jnp.float32)
+    low_up = lax.dot_general(rows, low_ups, contract, preferred_element_type=jnp.float32)
+    low_all = (jax.nn.silu(low_pre) * low_up).astype(jnp.bfloat16)
+
     packed = []
     for j in range(local_experts):
         hidden = swiglu(rows, dense_gate[j], dense_up[j])
-        low = swiglu(rows, delta_gate[j], delta_up[j])
+        low = low_all[:, j * low_width : (j + 1) * low_width]
         both = jnp.concatenate([hidden, low], axis=1)
         packed.append(
             jnp.dot(select[j], both, preferred_element_type=jnp.float32).astype(jnp.bfloat16)
@@ -91,8 +171,7 @@
         squares = jnp.sum(importance * deviation * deviation, axis=1)
         back = jnp.sum(jnp.where(pick[j], squares[:, None], 0.0), axis=0)
         total = total + weight[:, j] * back
-    total = lax.psum(total / D, ("exp", "base"))
-    return lax.dynamic_slice_in_dim(total, lax.axis_index("exp") * tok_rows, tok_rows)
+    return sum_over_group(total / D, groups, splits)
 
 
 def solution(mesh):

time: 205 us -> 177 us (0.86)
  blocking collectives: 70 us -> 38.6 us
  Pallas kernels: 0 us -> 8.43 us
  matrix products: 58.1 us -> 51.1 us
    psum x1 -> x0, blocking collectives: 31.3 us -> none  [shards(): total = lax.psum(total / D, ('exp', 'base'))]
    pallas_call x0 -> x1, Pallas kernels: none -> 8.43 us  [sum_over_group(): pl.pallas_call(functools.partial(sum_kernel, groups, splits), out_shape=j...]
    dot_general x9 -> x5, matrix products: 18.7 us -> 12 us  [swiglu(): gate_pre = jnp.dot(rows, gate_w, preferred_element_type=jnp.float32)]
    dot_general x8 -> x4, matrix products: 20.1 us -> 15 us  [swiglu(): up_pre = jnp.dot(rows, up_w, preferred_element_type=jnp.float32)]
    dot_general x0 -> x2, matrix products: none -> 4.92 us  [the longest x1 3.55 us: shards(): lax.dot_general(rows, low_gates, contract, preferred_element_type=jnp.flo...]
where the time goes in v2:
time: 177 us; the launch traced here: 176 us
  waiting for transfers between devices  55.4 us (31%)
  matrix products  51.1 us (29%)
  blocking collectives  38.6 us (22%)
  between operations  15.3 us (9%)
  Pallas kernels  8.43 us (5%)
  local copies, waits for them, and re-layouts  5.76 us (3%)
    all_gather x1, waiting for transfers between devices, shards(): full = lax.all_gather(sent, 'base', axis=0, tiled=False)  40.1 us
    all_gather x1, blocking collectives, shards(): own_rows = lax.all_gather(tokens, 'base', axis=1, tiled=True)  23.5 us
    all_gather x1, waiting for transfers between devices, shards(): rows = lax.all_gather(own_rows, 'exp', axis=0, tiled=True)  15.3 us
    dot_general x4, matrix products, swiglu(): up_pre = jnp.dot(rows, up_w, preferred_element_type=jnp.float32)  15 us
    dot_general x5, matrix products, swiglu(): gate_pre = jnp.dot(rows, gate_w, preferred_element_type=jnp.float32)  12 us
    all_gather x1, blocking collectives, shards(): base_all = lax.all_gather(base_own, 'exp', axis=0, tiled=True)  9.51 us
    pallas_call x1, Pallas kernels, sum_over_group(): pl.pallas_call(functools.partial(sum_kernel, groups, splits), out_shape=j...  8.43 us
    dot_general x4, matrix products, shards(): jnp.dot(hid, dense_down[j], preferred_element_type=jnp.float32)  7.95 us
  transfers between devices with their start and end apart: 3, of which 2 were waited for; matrix products, arithmetic and copies ran while one was open for 24% of the time, Pallas kernels for 0%

profile of v2, /device:TPU:0, one launch (start us, length us, event | category | flops | bytes accessed | tf_op | source)
XLA Modules:
  0.0 176.2 jit_solution(17845312094961861251)
XLA Ops:
  7.4 23.5 %all_gather.19 = bf16[64,7168]{1,0:T(8,128)(2,1)} all-gather(bf16[64,1792]{1,0:T(8,128)(2,1)} %param.13), channel_id=1, replica_groups=mesh['grp'=2,'exp'=4,'base'=4] {'base'}, dimensions={1}, use_global_device_ids=true | all-gather | bytes 1146880 | tf_op jit(solution)/shard_map/all_gather | solution.py:117
  30.9 0.0 all-gather.5.cloned.1.call-update
  30.9 0.0 reduce-scatter.2.cloned.1.call-start
  31.0 3.1 %fusion.184 = f32[64,256]{1,0:T(8,128)S(1)} fusion(bf16[64,7168]{1,0:T(8,128)(2,1)} %all_gather.19, bf16[7168,256]{1,0:T(8,128)(2,1)} %param.23), kind=kOutput, calls=%fused_computation.247 | convolution fusion | flops 234881024 | bytes 4653056 | tf_op jit(solution)/shard_map/dot_general | solution.py:83
  34.1 6.6 %convolution_convert_fusion = bf16[64,7168]{1,0:T(8,128)(2,1)} fusion(bf16[256,7168]{1,0:T(8,128)(2,1)} %param.25, bf16[64,7168]{1,0:T(8,128)(2,1)S(1)} %copy-done.2, bf16[7168,256]{1,0:T(8,128)(2,1)} %param.24, f32[64,256]{1,0:T(8,128)S(1)} %fusion.184), kind=kOutput, calls=%fused_computation | convolution fusion | flops 470319104 | bytes 9240576 | tf_op jit(solution)/shard_map/dot_general | solution.py:137
  40.8 0.0 reduce-scatter.2.cloned.1.call-update
  40.8 0.0 all-gather.7.cloned.1.call-start
  40.9 5.5 %all-gather.1 = s32[4,64,16]{1,2,0:T(8,128)S(1)} all-gather(s32[1,64,16]{1,2,0:T(8,128)S(1)} %add_bitcast_fusion), channel_id=1, replica_groups=mesh['grp'=2,'exp'=4,'base'=4] {'exp'}, dimensions={0}, use_global_device_ids=true | all-gather | bytes 20480 | tf_op jit(solution)/shard_map/all_gather | solution.py:114
  46.5 0.1 reshape.134
  46.5 0.1 compare_reduce_fusion
  46.6 0.2 fusion.79
  46.9 0.1 iota_compare_fusion
  47.0 15.3 %all-gather.5.cloned.1.call-done = bf16[256,7168]{1,0:T(8,128)(2,1)} async-done(((bf16[64,7168]{1,0:T(8,128)(2,1)}), bf16[256,7168]{1,0:T(8,128)(2,1)}) %all-gather.5.cloned.1.call-update) | async-done | bytes 3670032 | tf_op jit(solution)/shard_map/all_gather | solution.py:118
  62.3 3.6 %fusion.183 = f32[256,128]{0,1:T(8,128)S(1)} fusion(bf16[256,7168]{1,0:T(8,128)(2,1)} %all-gather.5.cloned.1.call-done, bf16[128,7168]{1,0:T(8,128)(2,1)S(1)} %bitcast.197), kind=kOutput, calls=%fused_computation.246 | convolution fusion | flops 469762048 | bytes 5636096 | tf_op jit(solution)/shard_map/dot_general | solution.py:146
  65.9 0.2 copy-done.8
  66.1 1.4 fusion.76
  67.4 0.0 slice-start.2
  67.5 3.8 %fusion.10 = f32[256,256]{0,1:T(8,128)S(1)} fusion(bf16[256,7168]{1,0:T(8,128)(2,1)S(1)} %copy-done.3, bf16[4,7168,256]{2,1,0:T(8,128)(2,1)} %param.17), kind=kOutput, calls=%fused_computation.11 | convolution fusion | flops 939524096 | bytes 7602176 | tf_op jit(solution)/shard_map/dot_general | solution.py:83
  71.3 0.0 slice-start.3
  71.3 3.9 %fusion.60 = bf16[256,256]{0,1:T(8,128)(2,1)S(1)} fusion(bf16[256,7168]{1,0:T(8,128)(2,1)S(1)} %copy-done.3, bf16[4,7168,256]{2,1,0:T(8,128)(2,1)} %param.18, f32[256,256]{0,1:T(8,128)S(1)} %fusion.10), kind=kOutput, calls=%fused_computation.69 | convolution fusion | flops 939917312 | bytes 7733248 | tf_op jit(solution)/shard_map/dot_general | solution.py:84
  75.2 0.2 fusion.75
  75.5 1.6 fusion.14
  77.1 3.7 %fusion.63 = bf16[256,256]{0,1:T(8,128)(2,1)S(1)} fusion(bf16[256,7168]{1,0:T(8,128)(2,1)S(1)} %copy-done.3, bf16[4,7168,256]{2,1,0:T(8,128)(2,1)} %param.18, f32[256,256]{0,1:T(8,128)S(1)} %fusion.14), kind=kOutput, calls=%fused_computation.70 | convolution fusion | flops 939917312 | bytes 7733248 | tf_op jit(solution)/shard_map/dot_general | solution.py:84
  80.8 0.2 fusion.74
  81.1 1.6 fusion.18
  82.7 3.7 %fusion.66 = bf16[256,256]{0,1:T(8,128)(2,1)S(1)} fusion(bf16[256,7168]{1,0:T(8,128)(2,1)S(1)} %copy-done.3, bf16[4,7168,256]{2,1,0:T(8,128)(2,1)} %param.18, f32[256,256]{0,1:T(8,128)S(1)} %fusion.18), kind=kOutput, calls=%fused_computation.71 | convolution fusion | flops 939917312 | bytes 7733248 | tf_op jit(solution)/shard_map/dot_general | solution.py:84
  86.4 0.2 fusion.73
  86.6 1.8 %fusion.22 = f32[256,256]{0,1:T(8,128)S(1)} fusion(bf16[256,7168]{1,0:T(8,128)(2,1)S(1)} %copy-done.3, bf16[4,7168,256]{2,1,0:T(8,128)(2,1)S(1)} %bitcast.201), kind=kOutput, calls=%fused_computation.23 | convolution fusion | flops 939524096 | bytes 7602176 | tf_op jit(solution)/shard_map/dot_general | solution.py:83
  88.5 3.7 %fusion.69 = bf16[256,256]{0,1:T(8,128)(2,1)S(1)} fusion(bf16[256,7168]{1,0:T(8,128)(2,1)S(1)} %copy-done.3, bf16[4,7168,256]{2,1,0:T(8,128)(2,1)} %param.18, f32[256,256]{0,1:T(8,128)S(1)} %fusion.22), kind=kOutput, calls=%fused_computation.72 | convolution fusion | flops 939917312 | bytes 7733248 | tf_op jit(solution)/shard_map/dot_general | solution.py:84
  92.2 0.2 fusion.72
  92.4 1.0 pad_maximum_fusion
  93.4 0.0 all-gather.7.cloned.1.call-update
  93.4 0.1 fusion.166
  93.6 0.1 squeeze.179
  93.6 0.1 squeeze.224
  93.7 0.1 squeeze.213
  93.8 0.1 squeeze.202
  93.9 9.5 %all_gather.23 = bf16[256,1792]{1,0:T(8,128)(2,1)S(1)} all-gather(bf16[64,1792]{1,0:T(8,128)(2,1)} %reduce-scatter.2.cloned.1.call-done), channel_id=1, replica_groups=mesh['grp'=2,'exp'=4,'base'=4] {'exp'}, dimensions={0}, use_global_device_ids=true | all-gather | bytes 1146880 | tf_op jit(solution)/shard_map/all_gather | solution.py:141
  103.4 40.1 %all-gather.7.cloned.1.call-done = bf16[16,192,288]{2,1,0:T(8,128)(2,1)} async-done(((bf16[4,192,288]{2,1,0:T(8,128)(2,1)}), bf16[16,192,288]{2,1,0:T(8,128)(2,1)}) %all-gather.7.cloned.1.call-update) | async-done | bytes 1769488 | tf_op jit(solution)/shard_map/all_gather | solution.py:159
  143.5 1.2 slice_bitcast_fusion.39
  144.7 1.7 slice_bitcast_fusion.23
  146.5 0.0 slice-start.5
  146.5 3.1 %fusion.4 = f32[192,1792]{1,0:T(8,128)S(1)} fusion(bf16[4,1024,1792]{2,1,0:T(8,128)(2,1)} %param.19, bf16[192,256]{1,0:T(8,128)(2,1)S(1)} %get-tuple-element.38, bf16[192,256]{1,0:T(8,128)(2,1)S(1)} %get-tuple-element.39, bf16[192,256]{1,0:T(8,128)(2,1)S(1)} %get-tuple-element.40, bf16[192,256]{1,0:T(8,128)(2,1)S(1)} %get-tuple-element.29), kind=kOutput, calls=%fused_computation.5 | convolution fusion | flops 706215936 | bytes 5439488 | tf_op jit(solution)/shard_map/dot_general | solution.py:165
  149.6 0.4 fusion.39
  150.0 0.0 slice-start.6
  150.0 0.5 fusion.45
  150.4 0.0 slice-start.7
  150.5 3.1 %fusion = f32[192,1792]{1,0:T(8,128)S(1)} fusion(bf16[4,1024,1792]{2,1,0:T(8,128)(2,1)} %param.19, bf16[192,256]{1,0:T(8,128)(2,1)S(1)} %get-tuple-element.30, bf16[192,256]{1,0:T(8,128)(2,1)S(1)} %get-tuple-element.31, bf16[192,256]{1,0:T(8,128)(2,1)S(1)} %get-tuple-element.32, bf16[192,256]{1,0:T(8,128)(2,1)S(1)} %get-tuple-element.33), kind=kOutput, calls=%fused_computation.1 | convolution fusion | flops 706215936 | bytes 5439488 | tf_op jit(solution)/shard_map/dot_general | solution.py:165
  153.6 0.4 fusion.43
  154.0 0.5 fusion.47
  154.5 0.9 fusion.2
  155.4 0.4 fusion.41
  155.8 0.5 fusion.46
  156.3 0.9 fusion.6
  157.2 0.4 fusion.37
  157.6 0.5 fusion.44
  158.0 0.2 select_reduce_fusion.3
  158.2 0.1 reduce_sum.92
  158.3 0.1 reduce_sum.101
  158.4 0.1 reduce_sum.98
  158.5 0.1 reduce_sum.95
  158.6 0.6 pad.4.part_ref
  159.2 8.4 %shard_map.127 = f32[8,128]{1,0:T(8,128)} custom-call(f32[4,8,128]{2,1,0:T(8,128)} %pad.4.part_ref), custom_call_target="tpu_custom_call" | custom-call | tf_op jit(solution)/shard_map/pallas_call | solution.py:67
  167.6 1.2 slice_bitcast_fusion.44
  (41 shorter events, 0.2 us)
Async XLA Ops:
  7.4 54.9 %copy-start = (bf16[4,7168,32]{1,2,0:T(8,128)(2,1)S(1)}, bf16[4,7168,32]{1,2,0:T(8,128)(2,1)}, u32[]{:S(2)}) copy-start(bf16[4,7168,32]{1,2,0:T(8,128)(2,1)} %param.20) | copy-start | bytes 5505028
  7.4 54.9 %all-gather.5.cloned.1.call-start = ((), (), s32[]{:S(2)}) async-start(), calls=%async_computation.1 | async-start | bytes 4587520 | tf_op jit(solution)/shard_map/all_gather | solution.py:118
  30.9 3.2 %copy-start.2 = (bf16[64,7168]{1,0:T(8,128)(2,1)S(1)}, bf16[64,7168]{1,0:T(8,128)(2,1)}, u32[]{:S(2)}) copy-start(bf16[64,7168]{1,0:T(8,128)(2,1)} %all_gather.19) | copy-start | bytes 2752516
  30.9 62.9 %reduce-scatter.2.cloned.1.call-start = ((), (), s32[]{:S(2)}) async-start(), calls=%async_computation.2 | async-start | bytes 1146880 | tf_op jit(solution)/shard_map/reduce_scatter | solution.py:138
  34.1 6.8 %copy-start.6 = (s32[64,8]{0,1:T(8,128)S(1)}, s32[64,8]{0,1:T(8,128)}, u32[]{:S(2)}) copy-start(s32[64,8]{0,1:T(8,128)} %param.15) | copy-start | bytes 6148
  34.1 6.8 %copy-start.7 = (s32[64,8]{0,1:T(8,128)S(1)}, s32[64,8]{0,1:T(8,128)}, u32[]{:S(2)}) copy-start(s32[64,8]{0,1:T(8,128)} %param.14) | copy-start | bytes 6148
  40.8 102.7 %all-gather.7.cloned.1.call-start = ((), (), s32[]{:S(2)}) async-start(), calls=%async_computation.3 | async-start | bytes 2949120 | tf_op jit(solution)/shard_map/all_gather | solution.py:159
  62.3 3.6 %copy-start.3 = (bf16[256,7168]{1,0:T(8,128)(2,1)S(1)}, bf16[256,7168]{1,0:T(8,128)(2,1)}, u32[]{:S(2)}) copy-start(bf16[256,7168]{1,0:T(8,128)(2,1)} %all-gather.5.cloned.1.call-done) | copy-start | bytes 11010052
  62.3 3.8 %copy-start.8 = (bf16[4,7168,32]{1,2,0:T(8,128)(2,1)S(1)}, bf16[4,7168,32]{1,2,0:T(8,128)(2,1)}, u32[]{:S(2)}) copy-start(bf16[4,7168,32]{1,2,0:T(8,128)(2,1)} %param.21) | copy-start | bytes 5505028
  62.3 13.2 %slice-start = ((s8[14680064]{0:T(1024)(128)(4,1)}), s8[4194304]{0:T(1024)(128)(4,1)S(1)}, s32[]{:S(2)}) async-start(s8[14680064]{0:T(1024)(128)(4,1)} %bitcast.200), calls=%async_computation.4 | async-start | bytes 8388608
  66.1 9.4 %slice-start.1 = ((s8[14680064]{0:T(1024)(128)(4,1)}), s8[4194304]{0:T(1024)(128)(4,1)S(1)}, s32[]{:S(2)}) async-start(s8[14680064]{0:T(1024)(128)(4,1)} %bitcast.200), calls=%async_computation.5 | async-start | bytes 8388608
  67.4 8.0 %slice-start.2 = ((s8[14680064]{0:T(1024)(128)(4,1)}), s8[4194304]{0:T(1024)(128)(4,1)S(1)}, s32[]{:S(2)}) async-start(s8[14680064]{0:T(1024)(128)(4,1)} %bitcast.200), calls=%async_computation.6 | async-start | bytes 8388608
  71.3 4.2 %slice-start.3 = ((s8[14680064]{0:T(1024)(128)(4,1)}), s8[2097152]{0:T(1024)(128)(4,1)S(1)}, s32[]{:S(2)}) async-start(s8[14680064]{0:T(1024)(128)(4,1)} %bitcast.200), calls=%async_computation.7 | async-start | bytes 4194304
  144.7 9.7 %slice-start.4 = ((s8[14680064]{0:T(1024)(128)(4,1)}), s8[4194304]{0:T(1024)(128)(4,1)S(1)}, s32[]{:S(2)}) async-start(s8[14680064]{0:T(1024)(128)(4,1)} %bitcast.202), calls=%async_computation.8 | async-start | bytes 8388608
  146.4 3.1 %copy-start.4 = (bf16[4,128,1792]{2,1,0:T(8,128)(2,1)S(1)}, bf16[4,128,1792]{2,1,0:T(8,128)(2,1)}, u32[]{:S(2)}) copy-start(bf16[4,128,1792]{2,1,0:T(8,128)(2,1)} %param.22) | copy-start | bytes 5505028
  146.5 3.5 %copy-start.5 = (f32[1792]{0:T(1024)S(1)}, f32[1792]{0:T(1024)}, u32[]{:S(2)}) copy-start(f32[1792]{0:T(1024)} %param.16) | copy-start | bytes 21508
  146.5 8.0 %slice-start.5 = ((s8[14680064]{0:T(1024)(128)(4,1)}), s8[4194304]{0:T(1024)(128)(4,1)S(1)}, s32[]{:S(2)}) async-start(s8[14680064]{0:T(1024)(128)(4,1)} %bitcast.202), calls=%async_computation.9 | async-start | bytes 8388608
  150.0 4.5 %slice-start.6 = ((s8[14680064]{0:T(1024)(128)(4,1)}), s8[4194304]{0:T(1024)(128)(4,1)S(1)}, s32[]{:S(2)}) async-start(s8[14680064]{0:T(1024)(128)(4,1)} %bitcast.202), calls=%async_computation.10 | async-start | bytes 8388608
  150.4 4.0 %slice-start.7 = ((s8[14680064]{0:T(1024)(128)(4,1)}), s8[2097152]{0:T(1024)(128)(4,1)S(1)}, s32[]{:S(2)}) async-start(s8[14680064]{0:T(1024)(128)(4,1)} %bitcast.202), calls=%async_computation.11 | async-start | bytes 4194304
  156.3 12.5 %copy-start.1 = (bf16[4,7168,32]{1,2,0:T(8,128)(2,1)S(1)}, bf16[4,7168,32]{1,2,0:T(8,128)(2,1)}, u32[]{:S(2)}) copy-start(bf16[4,7168,32]{1,2,0:T(8,128)(2,1)} %param.20) | copy-start | bytes 5505028
Sparse Core Ops, SparseCore 0:
  31.1 31.1 all-gather.4
Sparse Core Ops, SparseCore 1:
  40.9 24.3 reduce-scatter.1
  93.5 50.0 all-gather.6

commit v3 on v2

--- a/solution.py
+++ b/solution.py
@@ -77,6 +77,210 @@
         compiler_params=pltpu.CompilerParams(collective_id=0, has_side_effects=True),
     )(part)
     return out[0, :tok_rows]
+
+
+def tile_of(width, sizes):
+    return next((size for size in sizes if width % size == 0), width)
+
+
+def expert_kernel(
+    splits,
+    rows_ref,
+    select_ref,
+    low_ref,
+    gate_ref,
+    up_ref,
+    down_ref,
+    low_down_ref,
+    out_ref,
+    gate_buf,
+    up_buf,
+    down_buf,
+    hidden,
+    lows,
+    gate_acc,
+    up_acc,
+    load_sem,
+    down_sem,
+    send_sem,
+    recv_sem,
+):
+    experts, depth, width = gate_ref.shape
+    local_width = down_ref.shape[2]
+    low_width = low_ref.shape[1] // experts
+    last = splits - 1
+    me = lax.axis_index("base")
+    barrier = pltpu.get_barrier_semaphore()
+
+    def load(j):
+        slot = j % 2
+        return (
+            pltpu.make_async_copy(gate_ref.at[j], gate_buf.at[slot], load_sem.at[0, slot]),
+            pltpu.make_async_copy(up_ref.at[j], up_buf.at[slot], load_sem.at[1, slot]),
+        )
+
+    def load_down(j):
+        return pltpu.make_async_copy(down_ref.at[j], down_buf.at[j], down_sem.at[j])
+
+    for j in range(min(2, experts)):
+        for copy in load(j):
+            copy.start()
+
+    for off in range(1, splits):
+        pl.semaphore_signal(
+            barrier,
+            inc=1,
+            device_id={"base": lax.rem(me + off, splits)},
+            device_id_type=pl.DeviceIdType.MESH,
+        )
+    pl.semaphore_wait(barrier, last)
+
+    def passing(item, source, way):
+        step = 1 if way == 0 else -1
+        ref = lows.at[source] if item == experts else hidden.at[source, item]
+        return pltpu.make_async_remote_copy(
+            src_ref=ref,
+            dst_ref=ref,
+            send_sem=send_sem.at[way, source, item],
+            recv_sem=recv_sem.at[source, item],
+            device_id={"base": me + step},
+            device_id_type=pl.DeviceIdType.MESH,
+        )
+
+    def relay(item, far):
+        if far == 0:
+            for way, inside in ((0, me < last), (1, me > 0)):
+
+                @pl.when(inside)
+                def _(way=way):
+                    passing(item, me, way).start()
+
+            return
+        for way, source, inside, on in (
+            (0, me - far, me >= far, me < last),
+            (1, me + far, me + far <= last, me > 0),
+        ):
+
+            @pl.when(inside)
+            def _(way=way, source=source):
+                passing(item, source, way).wait_recv()
+
+            @pl.when(jnp.logical_and(inside, on))
+            def _(way=way, source=source):
+                passing(item, source, way).start()
+
+    lows[me] = low_ref[...]
+    relay(experts, 0)
+
+    chunk = tile_of(depth, (1024, 512, 256, 128))
+    tile = tile_of(local_width, (256, 128))
+
+    def first_half(j):
+        for copy in load(j):
+            copy.wait()
+        slot = j % 2
+        gate_acc[...] = jnp.zeros_like(gate_acc)
+        up_acc[...] = jnp.zeros_like(up_acc)
+
+        @pl.loop(0, depth // chunk)
+        def _(c):
+            part = pl.ds(pl.multiple_of(c * chunk, chunk), chunk)
+            block = rows_ref[:, part]
+            gate_acc[...] += jnp.dot(
+                block, gate_buf[slot, part, :], preferred_element_type=jnp.float32
+            )
+            up_acc[...] += jnp.dot(block, up_buf[slot, part, :], preferred_element_type=jnp.float32)
+
+        if j + 2 < experts:
+            for copy in load(j + 2):
+                copy.start()
+        load_down(j).start()
+        value = gate_acc[...]
+        both = (value / (1.0 + jnp.exp(-value)) * up_acc[...]).astype(jnp.bfloat16)
+        hidden[me, j] = jnp.dot(
+            select_ref[j], both, preferred_element_type=jnp.float32
+        ).astype(jnp.bfloat16)
+
+    def second_half(j):
+        load_down(j).wait()
+        picked = []
+        for b in range(splits):
+            chosen = jnp.dot(select_ref[j], lows[b], preferred_element_type=jnp.float32)
+            picked.append(chosen[:, j * low_width : (j + 1) * low_width].astype(jnp.bfloat16))
+
+        @pl.loop(0, local_width // tile)
+        def _(c):
+            part = pl.ds(pl.multiple_of(c * tile, tile), tile)
+            total = jnp.zeros((out_ref.shape[1], tile), jnp.float32)
+            for b in range(splits):
+                total += jnp.dot(
+                    hidden[b, j],
+                    down_buf[j, b * width : (b + 1) * width, part],
+                    preferred_element_type=jnp.float32,
+                )
+            for b in range(splits):
+                total -= jnp.dot(
+                    picked[b],
+                    low_down_ref[j, b * low_width : (b + 1) * low_width, part],
+                    preferred_element_type=jnp.float32,
+                )
+            out_ref[j, :, part] = total.astype(jnp.bfloat16)
+
+    for step in range(experts + last):
+        if step < experts:
+            first_half(step)
+            relay(step, 0)
+        for far in range(1, splits):
+            if far == step + 1:
+                relay(experts, far)
+            if 0 <= step - far < experts:
+                relay(step - far, far)
+        if step >= last:
+            second_half(step - last)
+
+    for item in range(experts + 1):
+        for source in range(splits):
+            for way, inside in (
+                (0, jnp.logical_and(me >= source, me < last)),
+                (1, jnp.logical_and(me <= source, me > 0)),
+            ):
+
+                @pl.when(inside)
+                def _(item=item, source=source, way=way):
+                    passing(item, source, way).wait_send()
+
+
+def run_experts(rows, select, low_all, gate, up, down, low_down, splits):
+    experts, depth, width = gate.shape
+    slots = select.shape[1]
+    all_rows = rows.shape[0]
+    local_width = down.shape[2]
+    vmem, hbm = pl.BlockSpec(memory_space=pltpu.VMEM), pl.BlockSpec(memory_space=pl.ANY)
+    flops = 2 * experts * (2 * all_rows * depth * width + slots * splits * width * local_width)
+    moved = 2 * experts * (2 * depth * width + splits * width * local_width)
+    return pl.pallas_call(
+        functools.partial(expert_kernel, splits),
+        out_shape=jax.ShapeDtypeStruct((experts, slots, local_width), jnp.bfloat16),
+        in_specs=[vmem, vmem, vmem, hbm, hbm, hbm, vmem],
+        out_specs=vmem,
+        scratch_shapes=[
+            pltpu.VMEM((2, depth, width), jnp.bfloat16),
+            pltpu.VMEM((2, depth, width), jnp.bfloat16),
+            pltpu.VMEM(down.shape, jnp.bfloat16),
+            pltpu.VMEM((splits, experts, slots, width), jnp.bfloat16),
+            pltpu.VMEM((splits,) + low_all.shape, jnp.bfloat16),
+            pltpu.VMEM((all_rows, width), jnp.float32),
+            pltpu.VMEM((all_rows, width), jnp.float32),
+            pltpu.SemaphoreType.DMA((2, 2)),
+            pltpu.SemaphoreType.DMA((experts,)),
+            pltpu.SemaphoreType.DMA((2, splits, experts + 1)),
+            pltpu.SemaphoreType.DMA((splits, experts + 1)),
+        ],
+        compiler_params=pltpu.CompilerParams(
+            collective_id=1, has_side_effects=True, vmem_limit_bytes=54 * 1024 * 1024
+        ),
+        cost_estimate=pl.CostEstimate(flops=flops, bytes_accessed=moved, transcendentals=0),
+    )(rows, select, low_all, gate, up, down, low_down)
 
 
 def swiglu(rows, gate_w, up_w):
@@ -106,7 +310,6 @@
     top_k = expert_ids.shape[1]
     local_experts = dense_gate.shape[0]
     capacity = tok_rows * top_k * 3 // (2 * local_experts * groups)
-    dense_width = dense_gate.shape[2]
     low_width = delta_gate.shape[2]
     all_rows = tok_rows * groups
     slots = capacity * groups
@@ -147,25 +350,13 @@
     low_up = lax.dot_general(rows, low_ups, contract, preferred_element_type=jnp.float32)
     low_all = (jax.nn.silu(low_pre) * low_up).astype(jnp.bfloat16)
 
-    packed = []
-    for j in range(local_experts):
-        hidden = swiglu(rows, dense_gate[j], dense_up[j])
-        low = low_all[:, j * low_width : (j + 1) * low_width]
-        both = jnp.concatenate([hidden, low], axis=1)
-        packed.append(
-            jnp.dot(select[j], both, preferred_element_type=jnp.float32).astype(jnp.bfloat16)
-        )
-    sent = jnp.stack(packed)
-    full = lax.all_gather(sent, "base", axis=0, tiled=False)
+    residuals = run_experts(
+        rows, select, low_all, dense_gate, dense_up, dense_down, delta_down, splits
+    )
 
     total = jnp.zeros((all_rows,), jnp.float32)
     for j in range(local_experts):
-        hid = jnp.concatenate([full[b, j, :, :dense_width] for b in range(splits)], axis=1)
-        low = jnp.concatenate([full[b, j, :, dense_width:] for b in range(splits)], axis=1)
-        residual = jnp.dot(hid, dense_down[j], preferred_element_type=jnp.float32) - jnp.dot(
-            low, delta_down[j], preferred_element_type=jnp.float32
-        )
-        residual = residual.astype(jnp.bfloat16).astype(jnp.float32)
+        residual = residuals[j].astype(jnp.float32)
         base_rows = jnp.dot(select[j], base_all, preferred_element_type=jnp.float32)
         deviation = residual - base_rows
         squares = jnp.sum(importance * deviation * deviation, axis=1)

time: 177 us -> 152 us (0.86)
  Pallas kernels: 8.43 us -> 55.3 us
  waiting for transfers between devices: 55.4 us -> 17.7 us
  matrix products: 51.1 us -> 18 us
  local copies, waits for them, and re-layouts: 5.76 us -> 3.27 us
  blocking collectives: 38.6 us -> 40.6 us
    pallas_call x0 -> x1, Pallas kernels: none -> 47.3 us  [run_experts(): pl.pallas_call(functools.partial(expert_kernel, splits), out_shape=jax.Sh...]
    all_gather x1 -> x0, waiting for transfers between devices: 40.1 us -> none  [shards(): full = lax.all_gather(sent, 'base', axis=0, tiled=False)]
    dot_general x16 -> x0, matrix products: 25.5 us -> none  [the longest x4 15 us: swiglu(): up_pre = jnp.dot(rows, up_w, preferred_element_type=jnp.float32)]
    reduce_scatter x1, waiting for transfers between devices: 0.01 us -> 17.2 us  [shards(): lax.psum_scatter(partial_value.astype(jnp.bfloat16), 'base', scatter_dime...]
    all_gather x1, waiting for transfers between devices: 15.3 us -> 0.01 us  [shards(): rows = lax.all_gather(own_rows, 'exp', axis=0, tiled=True)]
    dot_general x5 -> x1, matrix products: 12 us -> 3.08 us  [swiglu(): gate_pre = jnp.dot(rows, gate_w, preferred_element_type=jnp.float32)]
    squeeze x2 -> x0, local copies, waits for them, and re-layouts: 2.89 us -> none  [the longest x1 1.71 us: shards(): full[b, j, :, :dense_width]]
    all_gather x1, blocking collectives: 9.51 us -> 12.4 us  [shards(): base_all = lax.all_gather(base_own, 'exp', axis=0, tiled=True)]
  transfers between devices with their start and end apart: 3 -> 2, of which waited for: 2 -> 1; matrix products, arithmetic and copies ran while one was open for 24% -> 1% of each run, Pallas kernels for 0% -> 0%
where the time goes in v3:
time: 152 us; the launch traced here: 151 us
  Pallas kernels  55.3 us (36%)
  blocking collectives  40.6 us (27%)
  matrix products  18 us (12%)
  waiting for transfers between devices  17.7 us (12%)
  between operations  15 us (10%)
  local copies, waits for them, and re-layouts  3.27 us (2%)
    pallas_call x1, Pallas kernels, run_experts(): pl.pallas_call(functools.partial(expert_kernel, splits), out_shape=jax.Sh...  47.3 us
    all_gather x1, blocking collectives, shards(): own_rows = lax.all_gather(tokens, 'base', axis=1, tiled=True)  23.1 us
    reduce_scatter x1, waiting for transfers between devices, shards(): lax.psum_scatter(partial_value.astype(jnp.bfloat16), 'base', scatter_dime...  17.2 us
    all_gather x1, blocking collectives, shards(): base_all = lax.all_gather(base_own, 'exp', axis=0, tiled=True)  12.4 us
    pallas_call x1, Pallas kernels, sum_over_group(): pl.pallas_call(functools.partial(sum_kernel, groups, splits), out_shape=j...  8.06 us
    dot_general x1, matrix products, shards(): jnp.dot(shared, base_down, preferred_element_type=jnp.float32)  6.39 us
    all_gather x1, blocking collectives, shards(): lax.all_gather(jnp.concatenate([expert_ids, gate_q], axis=1), 'exp', axis...  5.18 us
    dot_general x1, matrix products, shards(): lax.dot_general(rows, low_gates, contract, preferred_element_type=jnp.flo...  3.29 us
  transfers between devices with their start and end apart: 2, of which 1 were waited for; matrix products, arithmetic and copies ran while one was open for 1% of the time, Pallas kernels for 0%

profile of v3, /device:TPU:0, one launch (start us, length us, event | category | flops | bytes accessed | tf_op | source)
XLA Modules:
  0.0 151.3 jit_solution(12507577123692401547)
XLA Ops:
  7.4 0.0 copy-start
  7.4 0.0 reduce-scatter.2.cloned.1.call-start
  7.4 23.1 %all_gather.13 = bf16[64,7168]{1,0:T(8,128)(2,1)S(1)} all-gather(bf16[64,1792]{1,0:T(8,128)(2,1)} %param.13), channel_id=1, replica_groups=mesh['grp'=2,'exp'=4,'base'=4] {'base'}, dimensions={1}, use_global_device_ids=true | all-gather | bytes 1146880 | tf_op jit(solution)/shard_map/all_gather | solution.py:320
  30.5 0.0 copy-start.3
  30.5 3.1 %fusion.24 = f32[64,256]{1,0:T(8,128)S(1)} fusion(bf16[64,7168]{1,0:T(8,128)(2,1)S(1)} %all_gather.13, bf16[7168,256]{1,0:T(8,128)(2,1)} %param.23), kind=kOutput, calls=%fused_computation.62 | convolution fusion | flops 234881024 | bytes 4653056 | tf_op jit(solution)/shard_map/dot_general | solution.py:287
  33.5 0.0 copy-done.3
  33.6 6.4 %convolution_convert_fusion = bf16[64,7168]{1,0:T(8,128)(2,1)} fusion(bf16[256,7168]{1,0:T(8,128)(2,1)} %param.25, bf16[64,7168]{1,0:T(8,128)(2,1)S(1)} %all_gather.13, bf16[7168,256]{1,0:T(8,128)(2,1)} %param.24, f32[64,256]{1,0:T(8,128)S(1)} %fusion.24), kind=kOutput, calls=%fused_computation | convolution fusion | flops 470319104 | bytes 9240576 | tf_op jit(solution)/shard_map/dot_general | solution.py:340
  39.9 0.0 copy-start.5
  39.9 0.0 copy-start.6
  39.9 0.0 reduce-scatter.2.cloned.1.call-update
  40.0 0.0 all-gather.3.cloned.1.call-start
  40.0 0.5 all-gather.3.cloned.1.call-update
  40.6 0.1 copy-done.5
  40.6 0.0 copy-done.6
  40.7 5.2 %all-gather = s32[4,64,16]{1,2,0:T(8,128)S(1)} all-gather(s32[1,64,16]{1,2,0:T(8,128)S(1)} %add_bitcast_fusion), channel_id=1, replica_groups=mesh['grp'=2,'exp'=4,'base'=4] {'exp'}, dimensions={0}, use_global_device_ids=true | all-gather | bytes 20480 | tf_op jit(solution)/shard_map/all_gather | solution.py:317
  45.8 0.1 reshape.145
  45.9 0.1 fusion.18
  46.1 0.1 squeeze.35
  46.2 0.1 squeeze.41
  46.2 0.1 squeeze.39
  46.3 0.1 squeeze.37
  46.4 0.1 compare_reduce_fusion
  46.5 0.2 fusion.7
  46.7 0.9 fusion.20
  47.7 17.2 %reduce-scatter.2.cloned.1.call-done = bf16[64,1792]{1,0:T(8,128)(2,1)} async-done(((bf16[64,7168]{1,0:T(8,128)(2,1)}), bf16[64,1792]{1,0:T(8,128)(2,1)}) %reduce-scatter.2.cloned.1.call-update) | async-done | bytes 229392 | tf_op jit(solution)/shard_map/reduce_scatter | solution.py:341
  64.8 12.4 %all_gather.15 = bf16[256,1792]{1,0:T(8,128)(2,1)S(1)} all-gather(bf16[64,1792]{1,0:T(8,128)(2,1)} %reduce-scatter.2.cloned.1.call-done), channel_id=1, replica_groups=mesh['grp'=2,'exp'=4,'base'=4] {'exp'}, dimensions={0}, use_global_device_ids=true | all-gather | bytes 1146880 | tf_op jit(solution)/shard_map/all_gather | solution.py:344
  77.2 0.0 all-gather.3.cloned.1.call-done.rows_ref
  77.2 0.0 copy-done
  77.2 0.0 copy-start.2
  77.2 0.0 copy-start.7
  77.2 3.3 %fusion.23 = f32[256,128]{1,0:T(8,128)S(1)} fusion(bf16[256,7168]{1,0:T(8,128)(2,1)} %all-gather.3.cloned.1.call-done.rows_ref, bf16[128,7168]{1,0:T(8,128)(2,1)S(1)} %bitcast.60), kind=kOutput, calls=%fused_computation.61 | convolution fusion | flops 469762048 | bytes 5636096 | tf_op jit(solution)/shard_map/dot_general | solution.py:349
  80.5 0.0 copy-done.2
  80.5 0.4 copy-done.7
  80.9 1.7 %fusion.4.low_ref = bf16[256,128]{1,0:T(8,128)(2,1)} fusion(bf16[256,7168]{1,0:T(8,128)(2,1)S(1)} %copy-done.2, bf16[128,7168]{1,0:T(8,128)(2,1)S(1)} %bitcast.61, f32[256,128]{1,0:T(8,128)S(1)} %fusion.23), kind=kOutput, calls=%fused_computation.14 | convolution fusion | flops 469958656 | bytes 5701632 | tf_op jit(solution)/shard_map/dot_general | solution.py:350
  82.7 0.0 copy-start.8
  82.7 47.3 %shard_map.127 = bf16[4,192,1792]{2,1,0:T(8,128)(2,1)} custom-call(bf16[256,7168]{1,0:T(8,128)(2,1)} %all-gather.3.cloned.1.call-done.rows_ref, bf16[4,192,256]{2,1,0:T(8,128)(2,1)} %get-tuple-element.15.select_ref, bf16[256,128]{1,0:T(8,128)(2,1)} %fusion.4.low_ref, bf16[4,7168,256]{2,1,0:T(8,128)(2,1)} %gate_ref.1, bf16[4,7168,256]{2,1,0:T(8,128)(2,1)} %up_ref.1, ...), custom_call_target="tpu_custom_call" | custom-call | flops 10334765056 | bytes 44040192 | tf_op jit(solution)/shard_map/pallas_call | solution.py:261
  129.9 0.0 copy-start.4
  130.0 0.0 copy-done.8
  130.0 1.8 %fusion.3 = f32[192]{0:T(256)S(1)} fusion(bf16[256,1792]{1,0:T(8,128)(2,1)S(1)} %all_gather.15, bf16[4,192,1792]{2,1,0:T(8,128)(2,1)} %shard_map.127, f32[1792]{0:T(1024)S(1)} %copy-done.8, pred[4,192,256]{2,1,0:T(32,128)(4,1)S(1)} %get-tuple-element.16), kind=kOutput, calls=%fused_computation.12 | convolution fusion | flops 177880896 | bytes 1663744 | tf_op jit(solution)/shard_map/dot_general | solution.py:360
  131.7 0.2 copy-done.4
  131.9 0.5 fusion.2
  132.4 0.0 copy-start.1
  132.4 0.5 fusion.1
  132.9 0.5 fusion
  133.4 0.2 select_reduce_fusion.3
  133.6 0.1 reduce_sum.92
  133.7 0.1 reduce_sum.98
  133.8 0.1 reduce_sum.95
  133.9 0.1 reduce_sum.101
  134.0 0.6 pad.4.part_ref
  134.6 8.1 %shard_map.128 = f32[8,128]{1,0:T(8,128)} custom-call(f32[4,8,128]{2,1,0:T(8,128)} %pad.4.part_ref), custom_call_target="tpu_custom_call" | custom-call | tf_op jit(solution)/shard_map/pallas_call | solution.py:67
  142.6 1.2 slice_bitcast_fusion.8
  143.8 0.0 copy-done.1
  (8 shorter events, 0.1 us)
Async XLA Ops:
  7.4 69.8 %copy-start = (bf16[4,7168,32]{1,2,0:T(8,128)(2,1)S(1)}, bf16[4,7168,32]{1,2,0:T(8,128)(2,1)}, u32[]{:S(2)}) copy-start(bf16[4,7168,32]{1,2,0:T(8,128)(2,1)} %param.20) | copy-start | bytes 5505028
  7.4 57.5 %reduce-scatter.2.cloned.1.call-start = ((), (), s32[]{:S(2)}) async-start(), calls=%async_computation.2 | async-start | bytes 1146880 | tf_op jit(solution)/shard_map/reduce_scatter | solution.py:341
  30.5 3.1 %copy-start.3 = (bf16[64,7168]{1,0:T(8,128)(2,1)}, bf16[64,7168]{1,0:T(8,128)(2,1)S(1)}, u32[]{:S(2)}) copy-start(bf16[64,7168]{1,0:T(8,128)(2,1)S(1)} %all_gather.13) | copy-start | bytes 2752516
  39.9 0.7 copy-start.5
  39.9 0.7 copy-start.6
  40.0 37.2 %all-gather.3.cloned.1.call-start = ((), (), s32[]{:S(2)}) async-start(), calls=%async_computation.1 | async-start | bytes 4587520 | tf_op jit(solution)/shard_map/all_gather | solution.py:321
  77.2 3.3 %copy-start.2 = (bf16[256,7168]{1,0:T(8,128)(2,1)S(1)}, bf16[256,7168]{1,0:T(8,128)(2,1)}, u32[]{:S(2)}) copy-start(bf16[256,7168]{1,0:T(8,128)(2,1)} %all-gather.3.cloned.1.call-done.rows_ref) | copy-start | bytes 11010052
  77.2 3.7 %copy-start.7 = (bf16[4,7168,32]{1,2,0:T(8,128)(2,1)S(1)}, bf16[4,7168,32]{1,2,0:T(8,128)(2,1)}, u32[]{:S(2)}) copy-start(bf16[4,7168,32]{1,2,0:T(8,128)(2,1)} %param.21) | copy-start | bytes 5505028
  82.7 47.3 %copy-start.8 = (f32[1792]{0:T(1024)S(1)}, f32[1792]{0:T(1024)}, u32[]{:S(2)}) copy-start(f32[1792]{0:T(1024)} %param.16) | copy-start | bytes 21508
  129.9 2.0 %copy-start.4 = (bf16[4,192,1792]{2,1,0:T(8,128)(2,1)S(1)}, bf16[4,192,1792]{2,1,0:T(8,128)(2,1)}, u32[]{:S(2)}) copy-start(bf16[4,192,1792]{2,1,0:T(8,128)(2,1)} %shard_map.127) | copy-start | bytes 8257540
  132.4 11.4 %copy-start.1 = (bf16[4,7168,32]{1,2,0:T(8,128)(2,1)S(1)}, bf16[4,7168,32]{1,2,0:T(8,128)(2,1)}, u32[]{:S(2)}) copy-start(bf16[4,7168,32]{1,2,0:T(8,128)(2,1)} %param.20) | copy-start | bytes 5505028
Sparse Core Ops, SparseCore 0:
  40.1 24.7 reduce-scatter.1
Sparse Core Ops, SparseCore 1:
  42.0 33.9 all-gather.2

commit v4 on v3

--- a/solution.py
+++ b/solution.py
@@ -85,6 +85,7 @@
 
 def expert_kernel(
     splits,
+    groups,
     rows_ref,
     select_ref,
     low_ref,
@@ -92,7 +93,9 @@
     up_ref,
     down_ref,
     low_down_ref,
+    base_ref,
     out_ref,
+    bases,
     gate_buf,
     up_buf,
     down_buf,
@@ -104,12 +107,15 @@
     down_sem,
     send_sem,
     recv_sem,
+    base_send,
+    base_recv,
 ):
     experts, depth, width = gate_ref.shape
     local_width = down_ref.shape[2]
     low_width = low_ref.shape[1] // experts
     last = splits - 1
     me = lax.axis_index("base")
+    own = lax.axis_index("exp")
     barrier = pltpu.get_barrier_semaphore()
 
     def load(j):
@@ -133,7 +139,28 @@
             device_id={"base": lax.rem(me + off, splits)},
             device_id_type=pl.DeviceIdType.MESH,
         )
-    pl.semaphore_wait(barrier, last)
+    for off in range(1, groups):
+        pl.semaphore_signal(
+            barrier,
+            inc=1,
+            device_id={"exp": lax.rem(own + off, groups)},
+            device_id_type=pl.DeviceIdType.MESH,
+        )
+    pl.semaphore_wait(barrier, last + groups - 1)
+
+    def base_copy(off, block):
+        return pltpu.make_async_remote_copy(
+            src_ref=base_ref,
+            dst_ref=bases.at[block],
+            send_sem=base_send.at[off],
+            recv_sem=base_recv.at[block],
+            device_id={"exp": lax.rem(own + off, groups)},
+            device_id_type=pl.DeviceIdType.MESH,
+        )
+
+    for off in range(1, groups):
+        base_copy(off, own).start()
+    bases[own] = base_ref[...]
 
     def passing(item, source, way):
         step = 1 if way == 0 else -1
@@ -238,6 +265,11 @@
         if step >= last:
             second_half(step - last)
 
+    for off in range(1, groups):
+        arrived = base_copy(off, lax.rem(own + off, groups))
+        arrived.wait_recv()
+        arrived.wait_send()
+
     for item in range(experts + 1):
         for source in range(splits):
             for way, inside in (
@@ -250,7 +282,7 @@
                     passing(item, source, way).wait_send()
 
 
-def run_experts(rows, select, low_all, gate, up, down, low_down, splits):
+def run_experts(rows, select, low_all, gate, up, down, low_down, base_own, splits, groups):
     experts, depth, width = gate.shape
     slots = select.shape[1]
     all_rows = rows.shape[0]
@@ -259,10 +291,13 @@
     flops = 2 * experts * (2 * all_rows * depth * width + slots * splits * width * local_width)
     moved = 2 * experts * (2 * depth * width + splits * width * local_width)
     return pl.pallas_call(
-        functools.partial(expert_kernel, splits),
-        out_shape=jax.ShapeDtypeStruct((experts, slots, local_width), jnp.bfloat16),
-        in_specs=[vmem, vmem, vmem, hbm, hbm, hbm, vmem],
-        out_specs=vmem,
+        functools.partial(expert_kernel, splits, groups),
+        out_shape=(
+            jax.ShapeDtypeStruct((experts, slots, local_width), jnp.bfloat16),
+            jax.ShapeDtypeStruct((groups,) + base_own.shape, jnp.bfloat16),
+        ),
+        in_specs=[vmem, vmem, vmem, hbm, hbm, hbm, vmem, vmem],
+        out_specs=(vmem, vmem),
         scratch_shapes=[
             pltpu.VMEM((2, depth, width), jnp.bfloat16),
             pltpu.VMEM((2, depth, width), jnp.bfloat16),
@@ -275,12 +310,14 @@
             pltpu.SemaphoreType.DMA((experts,)),
             pltpu.SemaphoreType.DMA((2, splits, experts + 1)),
             pltpu.SemaphoreType.DMA((splits, experts + 1)),
+            pltpu.SemaphoreType.DMA((groups,)),
+            pltpu.SemaphoreType.DMA((groups,)),
         ],
         compiler_params=pltpu.CompilerParams(
             collective_id=1, has_side_effects=True, vmem_limit_bytes=54 * 1024 * 1024
         ),
         cost_estimate=pl.CostEstimate(flops=flops, bytes_accessed=moved, transcendentals=0),
-    )(rows, select, low_all, gate, up, down, low_down)
+    )(rows, select, low_all, gate, up, down, low_down, base_own)
 
 
 def swiglu(rows, gate_w, up_w):
@@ -341,7 +378,6 @@
     base_own = lax.psum_scatter(
         partial_value.astype(jnp.bfloat16), "base", scatter_dimension=1, tiled=True
     )
-    base_all = lax.all_gather(base_own, "exp", axis=0, tiled=True)
 
     contract = (((1,), (1,)), ((), ()))
     low_gates = delta_gate.transpose(0, 2, 1).reshape(local_experts * low_width, -1)
@@ -350,9 +386,19 @@
     low_up = lax.dot_general(rows, low_ups, contract, preferred_element_type=jnp.float32)
     low_all = (jax.nn.silu(low_pre) * low_up).astype(jnp.bfloat16)
 
-    residuals = run_experts(
-        rows, select, low_all, dense_gate, dense_up, dense_down, delta_down, splits
+    residuals, bases = run_experts(
+        rows,
+        select,
+        low_all,
+        dense_gate,
+        dense_up,
+        dense_down,
+        delta_down,
+        base_own,
+        splits,
+        groups,
     )
+    base_all = bases.reshape(all_rows, local_width)
 
     total = jnp.zeros((all_rows,), jnp.float32)
     for j in range(local_experts):

time: 152 us -> 138 us (0.908)
  blocking collectives: 40.6 us -> 28.9 us
  waiting for transfers between devices: 17.7 us -> 14.3 us
  matrix products: 18 us -> 19.8 us
    reduce_scatter x1, waiting for transfers between devices: 17.2 us -> 0.01 us  [shards(): lax.psum_scatter(partial_value.astype(jnp.bfloat16), 'base', scatter_dime...]
    all_gather x1, waiting for transfers between devices: 0.01 us -> 14.3 us  [shards(): rows = lax.all_gather(own_rows, 'exp', axis=0, tiled=True)]
    all_gather x1 -> x0, blocking collectives: 12.4 us -> none  [shards(): base_all = lax.all_gather(base_own, 'exp', axis=0, tiled=True)]
    dot_general x4, matrix products: 3.25 us -> 4.79 us  [shards(): base_rows = jnp.dot(select[j], base_all, preferred_element_type=jnp.float32)]
  transfers between devices with their start and end apart: 2 -> 2, of which waited for: 1 -> 1; matrix products, arithmetic and copies ran while one was open for 1% -> 12% of each run, Pallas kernels for 0% -> 0%
where the time goes in v4:
time: 138 us
  Pallas kernels  55.3 us (40%)
  blocking collectives  28.9 us (21%)
  matrix products  19.8 us (14%)
  between operations  15 us (11%)
  waiting for transfers between devices  14.3 us (10%)
  local copies, waits for them, and re-layouts  3.26 us (2%)
    pallas_call x1, Pallas kernels, run_experts(): pl.pallas_call(functools.partial(expert_kernel, splits, groups), out_shap...  47.2 us
    all_gather x1, blocking collectives, shards(): own_rows = lax.all_gather(tokens, 'base', axis=1, tiled=True)  23.5 us
    all_gather x1, waiting for transfers between devices, shards(): rows = lax.all_gather(own_rows, 'exp', axis=0, tiled=True)  14.3 us
    pallas_call x1, Pallas kernels, sum_over_group(): pl.pallas_call(functools.partial(sum_kernel, groups, splits), out_shape=j...  8.06 us
    dot_general x1, matrix products, shards(): jnp.dot(shared, base_down, preferred_element_type=jnp.float32)  6.63 us
    all_gather x1, blocking collectives, shards(): lax.all_gather(jnp.concatenate([expert_ids, gate_q], axis=1), 'exp', axis...  5.34 us
    dot_general x4, matrix products, shards(): base_rows = jnp.dot(select[j], base_all, preferred_element_type=jnp.float32)  4.79 us
    dot_general x1, matrix products, shards(): lax.dot_general(rows, low_gates, contract, preferred_element_type=jnp.flo...  3.32 us
  transfers between devices with their start and end apart: 2, of which 1 were waited for; matrix products, arithmetic and copies ran while one was open for 12% of the time, Pallas kernels for 0%

profile of v4, /device:TPU:0, one launch (start us, length us, event | category | flops | bytes accessed | tf_op | source)
XLA Modules:
  0.0 138.0 jit_solution(11982625387903426348)
XLA Ops:
  7.4 0.0 copy-start
  7.4 0.0 all-gather.3.cloned.1.call-start
  7.4 23.5 %all_gather.10 = bf16[64,7168]{1,0:T(8,128)(2,1)} all-gather(bf16[64,1792]{1,0:T(8,128)(2,1)} %param.13), channel_id=1, replica_groups=mesh['grp'=2,'exp'=4,'base'=4] {'base'}, dimensions={1}, use_global_device_ids=true | all-gather | bytes 1146880 | tf_op jit(solution)/shard_map/all_gather | solution.py:357
  30.9 0.0 all-gather.3.cloned.1.call-update
  30.9 0.0 copy-start.2
  31.0 0.0 reduce-scatter.2.cloned.1.call-start
  31.0 3.1 %fusion.24 = f32[64,256]{1,0:T(8,128)S(1)} fusion(bf16[64,7168]{1,0:T(8,128)(2,1)} %all_gather.10, bf16[7168,256]{1,0:T(8,128)(2,1)} %param.23), kind=kOutput, calls=%fused_computation.62 | convolution fusion | flops 234881024 | bytes 4653056 | tf_op jit(solution)/shard_map/dot_general | solution.py:324
  34.1 0.0 copy-done.2
  34.1 0.0 copy-start.4
  34.1 0.0 copy-start.5
  34.1 6.6 %convolution_convert_fusion = bf16[64,7168]{1,0:T(8,128)(2,1)} fusion(bf16[256,7168]{1,0:T(8,128)(2,1)} %param.25, bf16[64,7168]{1,0:T(8,128)(2,1)S(1)} %copy-done.2, bf16[7168,256]{1,0:T(8,128)(2,1)} %param.24, f32[64,256]{1,0:T(8,128)S(1)} %fusion.24), kind=kOutput, calls=%fused_computation | convolution fusion | flops 470319104 | bytes 9240576 | tf_op jit(solution)/shard_map/dot_general | solution.py:377
  40.8 0.0 reduce-scatter.2.cloned.1.call-update
  40.8 0.0 copy-done.4
  40.8 0.0 copy-done.5
  40.8 5.3 %all-gather = s32[4,64,16]{1,2,0:T(8,128)S(1)} all-gather(s32[1,64,16]{1,2,0:T(8,128)S(1)} %add_bitcast_fusion), channel_id=1, replica_groups=mesh['grp'=2,'exp'=4,'base'=4] {'exp'}, dimensions={0}, use_global_device_ids=true | all-gather | bytes 20480 | tf_op jit(solution)/shard_map/all_gather | solution.py:354
  46.2 0.1 reshape.149
  46.3 0.1 fusion.18
  46.4 0.1 squeeze.41
  46.5 0.1 squeeze.39
  46.6 0.1 squeeze.37
  46.7 0.1 squeeze.35
  46.8 0.1 compare_reduce_fusion
  46.8 0.2 fusion.7
  47.1 0.9 fusion.20
  48.0 14.3 %all-gather.3.cloned.1.call-done.rows_ref = bf16[256,7168]{1,0:T(8,128)(2,1)} async-done(((bf16[64,7168]{1,0:T(8,128)(2,1)}), bf16[256,7168]{1,0:T(8,128)(2,1)}) %all-gather.3.cloned.1.call-update) | async-done | bytes 3670032 | tf_op jit(solution)/shard_map/all_gather | solution.py:358
  62.3 0.0 copy-done
  62.3 0.0 copy-start.3
  62.3 0.0 copy-start.7
  62.3 3.3 %fusion.23 = f32[256,128]{1,0:T(8,128)S(1)} fusion(bf16[256,7168]{1,0:T(8,128)(2,1)} %all-gather.3.cloned.1.call-done.rows_ref, bf16[128,7168]{1,0:T(8,128)(2,1)S(1)} %bitcast.61), kind=kOutput, calls=%fused_computation.61 | convolution fusion | flops 469762048 | bytes 5636096 | tf_op jit(solution)/shard_map/dot_general | solution.py:385
  65.7 0.0 copy-done.3
  65.7 0.4 copy-done.7
  66.1 1.7 %fusion.4.low_ref = bf16[256,128]{1,0:T(8,128)(2,1)} fusion(bf16[256,7168]{1,0:T(8,128)(2,1)S(1)} %copy-done.3, bf16[128,7168]{1,0:T(8,128)(2,1)S(1)} %bitcast.62, f32[256,128]{1,0:T(8,128)S(1)} %fusion.23), kind=kOutput, calls=%fused_computation.14 | convolution fusion | flops 469958656 | bytes 5701632 | tf_op jit(solution)/shard_map/dot_general | solution.py:386
  67.8 0.0 reduce-scatter.2.cloned.1.call-done.base_ref
  67.8 0.0 copy-start.9
  67.8 47.2 %shard_map.127 = (bf16[4,192,1792]{2,1,0:T(8,128)(2,1)}, bf16[4,64,1792]{2,1,0:T(8,128)(2,1)}) custom-call(bf16[256,7168]{1,0:T(8,128)(2,1)} %all-gather.3.cloned.1.call-done.rows_ref, bf16[4,192,256]{2,1,0:T(8,128)(2,1)} %get-tuple-element.19.select_ref, bf16[256,128]{1,0:T(8,128)(2,1)} %fusion.4.low_ref, bf16[4,7168,256]{2,1,0:T(8,128)(2,1)} %gate_ref.1, ...), custom_call_target="tpu_custom_call" | custom-call | flops 10334765056 | bytes 44040192 | tf_op jit(solution)/shard_map/pallas_call | solution.py:293
  115.1 0.0 copy-start.6
  115.1 0.0 copy-done.9
  115.1 2.0 %fusion = f32[192]{0:T(256)S(1)} fusion(bf16[256,1792]{1,0:T(8,128)(2,1)} %bitcast.63, bf16[4,192,1792]{2,1,0:T(8,128)(2,1)} %get-tuple-element.7, f32[1792]{0:T(1024)S(1)} %copy-done.9, pred[4,192,256]{2,1,0:T(32,128)(4,1)S(1)} %get-tuple-element.20), kind=kOutput, calls=%fused_computation.9 | convolution fusion | flops 177880896 | bytes 1663744 | tf_op jit(solution)/shard_map/dot_general | solution.py:406
  117.2 0.2 copy-done.6
  117.4 0.0 copy-start.8
  117.4 1.8 %fusion.2 = f32[192]{0:T(256)S(1)} fusion(bf16[256,1792]{1,0:T(8,128)(2,1)} %bitcast.64, bf16[4,192,1792]{2,1,0:T(8,128)(2,1)S(1)} %copy-done.6, f32[1792]{0:T(1024)S(1)} %copy-done.9, pred[4,192,256]{2,1,0:T(32,128)(4,1)S(1)} %get-tuple-element.20), kind=kOutput, calls=%fused_computation.11 | convolution fusion | flops 177880896 | bytes 1663744 | tf_op jit(solution)/shard_map/dot_general | solution.py:406
  119.1 0.0 copy-done.8
  119.1 0.0 copy-start.1
  119.2 0.5 fusion.1
  119.7 0.5 fusion.3
  120.2 0.2 select_reduce_fusion.3
  120.4 0.1 reduce_sum.101
  120.4 0.1 reduce_sum.98
  120.5 0.1 reduce_sum.95
  120.6 0.1 reduce_sum.92
  120.7 0.6 pad.4.part_ref
  121.3 8.1 %shard_map.128 = f32[8,128]{1,0:T(8,128)} custom-call(f32[4,8,128]{2,1,0:T(8,128)} %pad.4.part_ref), custom_call_target="tpu_custom_call" | custom-call | tf_op jit(solution)/shard_map/pallas_call | solution.py:67
  129.4 1.2 slice_bitcast_fusion.8
  130.6 0.0 copy-done.1
  (8 shorter events, 0.1 us)
Async XLA Ops:
  7.4 55.0 %copy-start = (bf16[4,7168,32]{1,2,0:T(8,128)(2,1)S(1)}, bf16[4,7168,32]{1,2,0:T(8,128)(2,1)}, u32[]{:S(2)}) copy-start(bf16[4,7168,32]{1,2,0:T(8,128)(2,1)} %param.20) | copy-start | bytes 5505028
  7.4 55.0 %all-gather.3.cloned.1.call-start = ((), (), s32[]{:S(2)}) async-start(), calls=%async_computation.1 | async-start | bytes 4587520 | tf_op jit(solution)/shard_map/all_gather | solution.py:358
  30.9 3.2 %copy-start.2 = (bf16[64,7168]{1,0:T(8,128)(2,1)S(1)}, bf16[64,7168]{1,0:T(8,128)(2,1)}, u32[]{:S(2)}) copy-start(bf16[64,7168]{1,0:T(8,128)(2,1)} %all_gather.10) | copy-start | bytes 2752516
  31.0 36.9 %reduce-scatter.2.cloned.1.call-start = ((), (), s32[]{:S(2)}) async-start(), calls=%async_computation.2 | async-start | bytes 1146880 | tf_op jit(solution)/shard_map/reduce_scatter | solution.py:378
  34.1 6.7 %copy-start.4 = (s32[64,8]{0,1:T(8,128)S(1)}, s32[64,8]{0,1:T(8,128)}, u32[]{:S(2)}) copy-start(s32[64,8]{0,1:T(8,128)} %param.15) | copy-start | bytes 6148
  34.1 6.7 %copy-start.5 = (s32[64,8]{0,1:T(8,128)S(1)}, s32[64,8]{0,1:T(8,128)}, u32[]{:S(2)}) copy-start(s32[64,8]{0,1:T(8,128)} %param.14) | copy-start | bytes 6148
  62.3 3.3 %copy-start.3 = (bf16[256,7168]{1,0:T(8,128)(2,1)S(1)}, bf16[256,7168]{1,0:T(8,128)(2,1)}, u32[]{:S(2)}) copy-start(bf16[256,7168]{1,0:T(8,128)(2,1)} %all-gather.3.cloned.1.call-done.rows_ref) | copy-start | bytes 11010052
  62.3 3.8 %copy-start.7 = (bf16[4,7168,32]{1,2,0:T(8,128)(2,1)S(1)}, bf16[4,7168,32]{1,2,0:T(8,128)(2,1)}, u32[]{:S(2)}) copy-start(bf16[4,7168,32]{1,2,0:T(8,128)(2,1)} %param.21) | copy-start | bytes 5505028
  67.8 47.3 %copy-start.9 = (f32[1792]{0:T(1024)S(1)}, f32[1792]{0:T(1024)}, u32[]{:S(2)}) copy-start(f32[1792]{0:T(1024)} %param.16) | copy-start | bytes 21508
  115.1 2.3 %copy-start.6 = (bf16[4,192,1792]{2,1,0:T(8,128)(2,1)S(1)}, bf16[4,192,1792]{2,1,0:T(8,128)(2,1)}, u32[]{:S(2)}) copy-start(bf16[4,192,1792]{2,1,0:T(8,128)(2,1)} %get-tuple-element.7) | copy-start | bytes 8257540
  117.4 1.8 %copy-start.8 = (bf16[4,64,1792]{2,1,0:T(8,128)(2,1)S(1)}, bf16[4,64,1792]{2,1,0:T(8,128)(2,1)}, u32[]{:S(2)}) copy-start(bf16[4,64,1792]{2,1,0:T(8,128)(2,1)} %get-tuple-element.8) | copy-start | bytes 2752516
  119.1 11.4 %copy-start.1 = (bf16[4,7168,32]{1,2,0:T(8,128)(2,1)S(1)}, bf16[4,7168,32]{1,2,0:T(8,128)(2,1)}, u32[]{:S(2)}) copy-start(bf16[4,7168,32]{1,2,0:T(8,128)(2,1)} %param.20) | copy-start | bytes 5505028
Sparse Core Ops, SparseCore 0:
  31.1 31.2 all-gather.2
Sparse Core Ops, SparseCore 1:
  40.9 24.4 reduce-scatter.1
